TPU v7x, 512 devices: a whole 4x8x8 slice. The times are simulated.
512 devices in a mesh: row: 64 (over z_lo, y, core), col: 8 (over z_hi, x).
Axes of the slice: x: 4, y: 8, z: 8 (z_hi: 2, z_lo: 4; z = z_hi * 4 + z_lo), core: 2. Of those that a mesh axis runs over, the one named last changes fastest.
Arguments:
- homolog_activations: bfloat16 [1024, 64, 256], P(('row', 'col')), may hold values from -6 to 6
- first_linear_matrix: bfloat16 [256, 32], replicated, may hold values from -0.375 to 0.375
- second_linear_matrix: bfloat16 [256, 32], replicated, may hold values from -0.375 to 0.375
- output_weight: bfloat16 [1024, 128], replicated, may hold values from -0.1875 to 0.1875
- output_bias: float32 [128], replicated, may hold values from -3 to 3
- pair_update_gradient: bfloat16 [1024, 1024, 128], P('row', 'col'), may hold values from -6 to 6
Outputs:
- pair_representation_update: bfloat16 [1024, 1024, 128], P('row', 'col')
- activation_sensitivity: bfloat16 [1024, 64, 256], P(('row', 'col'))
- output_weight_gradient: float32 [1024, 128], replicated
All inputs are finite; a program needn't handle non-finite values.
Results may differ from a plain program's by a relative error of at most 0.015.
Values may be sent and summed in bfloat16 or wider, within the bound.
A program may use at most 64 MiB of HBM per device.

v0:
```python
import jax
import jax.numpy as jnp
from jax import lax
from jax.sharding import PartitionSpec as P

EPSILON = 1e-05


def layer_normalize(homolog_activations):
    value_entries = homolog_activations.astype(jnp.float32)
    center = jnp.mean(value_entries, axis=-1, keepdims=True)
    spread = jnp.mean(jnp.square(value_entries - center), axis=-1, keepdims=True)
    reciprocal_spread_factor = lax.rsqrt(spread + EPSILON)
    return ((value_entries - center) * reciprocal_spread_factor, reciprocal_spread_factor)


def project(normed, weight):
    flat_rows = normed.reshape(-1, normed.shape[-1])
    result = jnp.dot(flat_rows, weight, preferred_element_type=jnp.float32).astype(jnp.bfloat16)
    return result.reshape(normed.shape[0], normed.shape[1] * weight.shape[1])


def standardizer_adjoint(standardized_sensitivity, rescaled_features, reciprocal_spread_factor):
    mean_grad = jnp.mean(standardized_sensitivity, axis=-1, keepdims=True)
    mean_cross = jnp.mean(standardized_sensitivity * rescaled_features, axis=-1, keepdims=True)
    return (
        reciprocal_spread_factor
        * (standardized_sensitivity - mean_grad - rescaled_features * mean_cross)
    ).astype(jnp.bfloat16)


def on_device(
    homolog_activations,
    first_linear_matrix,
    second_linear_matrix,
    output_weight,
    output_bias,
    pair_update_gradient,
):
    row_count = lax.axis_size("row")
    col_count = lax.axis_size("col")
    col_index = lax.axis_index("col")
    residues_per_device, alignment_depth, channel_count = homolog_activations.shape
    projection_width = first_linear_matrix.shape[1]
    flattened_width = alignment_depth * projection_width
    block_row_span = residues_per_device * col_count
    block_columns = residues_per_device * row_count
    total_res = block_columns * col_count
    rescaled_features, reciprocal_spread_factor = layer_normalize(homolog_activations)
    normed = rescaled_features.astype(jnp.bfloat16)
    left_own = project(normed, first_linear_matrix)
    right_own = project(normed, second_linear_matrix)
    left_tile_block = lax.all_gather(left_own, "col", axis=0, tiled=True)
    right_all = lax.all_gather(right_own, ("row", "col"), axis=0, tiled=True)
    right_tile_block = lax.dynamic_slice_in_dim(
        right_all, col_index * block_columns, block_columns, 0
    )
    left_triple = left_tile_block.reshape(block_row_span, alignment_depth, projection_width)
    right_triple = right_tile_block.reshape(block_columns, alignment_depth, projection_width)
    outer = (
        jnp.einsum("isc,jse->ijce", left_triple, right_triple, preferred_element_type=jnp.float32)
        / alignment_depth
    )
    outer = outer.astype(jnp.bfloat16).reshape(-1, projection_width * projection_width)
    pair_flat = jnp.dot(outer, output_weight, preferred_element_type=jnp.float32) + output_bias
    pair_representation_update = pair_flat.astype(jnp.bfloat16).reshape(
        block_row_span, block_columns, -1
    )
    cotangent = pair_update_gradient.reshape(-1, pair_update_gradient.shape[-1])
    grad_outer = jnp.dot(cotangent, output_weight.T, preferred_element_type=jnp.float32).astype(
        jnp.bfloat16
    )
    weight_part = jnp.dot(outer.T, cotangent, preferred_element_type=jnp.float32)
    grad_outer = grad_outer.reshape(
        block_row_span, block_columns, projection_width, projection_width
    )
    term = (
        jnp.einsum("ijce,jse->isc", grad_outer, right_triple, preferred_element_type=jnp.float32)
        / alignment_depth
    )
    left_own_grad = lax.psum_scatter(
        term.reshape(lax.axis_size("col") * residues_per_device, flattened_width).astype(
            jnp.bfloat16
        ),
        "col",
        scatter_dimension=0,
        tiled=True,
    ).astype(jnp.float32)
    right_partial = (
        jnp.einsum("ijce,isc->jse", grad_outer, left_triple, preferred_element_type=jnp.float32)
        / alignment_depth
    )
    right_partial = right_partial.reshape(block_columns, flattened_width)
    spread_back = lax.all_to_all(
        right_partial.astype(jnp.bfloat16), "col", split_axis=1, concat_axis=0, tiled=True
    ).astype(right_partial.dtype)
    right_rows_grad = lax.psum_scatter(spread_back, "row", scatter_dimension=0, tiled=True)
    right_own_grad = lax.all_to_all(right_rows_grad, "col", split_axis=0, concat_axis=1, tiled=True)
    weight_total = lax.psum(weight_part, ("row", "col"))
    output_weight_gradient = weight_total * (8.0 / total_res)
    left_flat = left_own_grad.reshape(-1, projection_width)
    right_flat = right_own_grad.reshape(-1, projection_width)
    standardized_sensitivity = jnp.dot(
        left_flat, first_linear_matrix.astype(jnp.float32).T, precision=lax.Precision.HIGHEST
    )
    standardized_sensitivity = standardized_sensitivity + jnp.dot(
        right_flat, second_linear_matrix.astype(jnp.float32).T, precision=lax.Precision.HIGHEST
    )
    activation_sensitivity = standardizer_adjoint(
        standardized_sensitivity.reshape(residues_per_device, alignment_depth, channel_count),
        rescaled_features,
        reciprocal_spread_factor,
    )
    return (pair_representation_update, activation_sensitivity, output_weight_gradient)


def solution(mesh):
    return jax.shard_map(
        on_device,
        mesh=mesh,
        in_specs=(P(("row", "col"), None, None), P(), P(), P(), P(), P("row", "col", None)),
        out_specs=(P("row", "col", None), P(("row", "col"), None, None), P()),
        check_vma=False,
    )
```

profile of v0, /device:TPU:1, one launch (start us, length us, event | category | flops | bytes accessed | tf_op | source)
XLA Modules:
  0.0 1901.5 jit_solution(2251007139465510050)
XLA Ops:
  8.0 0.0 copy-start
  8.0 0.0 reduce-scatter.2.cloned.1.call-start
  8.1 1.0 convert_reduce_fusion
  9.1 1.0 fusion.55
  10.1 0.9 fusion.50
  11.0 0.0 copy-done
  11.0 4.1 convolution_convert_fusion
  15.2 6.5 copy.47
  21.7 0.0 copy-start.4
  21.7 5.6 copy.66
  27.2 0.0 copy-done.4
  27.2 0.1 convolution_convert_fusion.1
  27.4 0.1 copy.43
  27.5 0.1 reshape.99
  27.6 42.2 %all-gather.1 = bf16[8,2,2048]{2,1,0:T(2,128)(2,1)S(1)} all-gather(bf16[1,2,2048]{2,1,0:T(2,128)(2,1)S(1)} %reshape.99), channel_id=1, replica_groups=mesh['row'=64,'col'=8] {'col'}, dimensions={0}, use_global_device_ids=true | all-gather | bytes 73728 | tf_op jit(solution)/shard_map/all_gather | solution.py:53
  69.9 0.2 reshape.88
  70.0 4.9 fusion.26
  75.0 0.3 copy.53
  75.3 20.2 %all_to_all.26 = bf16[128,8,256]{0,2,1:T(8,128)(2,1)S(1)} all-to-all(bf16[128,8,256]{0,2,1:T(8,128)(2,1)S(1)} %bitcast.87), channel_id=1, replica_groups=mesh['row'=64,'col'=8] {'col'}, dimensions={1} | all-to-all | bytes 1048576 | tf_op jit(solution)/shard_map/all_to_all | solution.py:94
  95.5 0.1 convert_bitcast_fusion
  95.6 1.4 copy.54
  97.0 0.0 reduce-scatter.2.cloned.1.call-update
  97.0 0.0 all-gather.4.cloned.1.call-start
  97.0 0.0 copy-done.5
  97.1 0.1 convolution_convert_fusion.2
  97.2 0.1 copy.41
  97.3 0.7 reshape.97
  98.0 0.0 all-gather.4.cloned.1.call-update
  98.1 282.0 %reduce-scatter.2.cloned.1.call-done = f32[16,256]{1,0:T(8,128)} async-done(((f32[1024,256]{1,0:T(8,128)}), f32[16,256]{1,0:T(8,128)}) %reduce-scatter.2.cloned.1.call-update) | async-done | bytes 16400 | tf_op jit(solution)/shard_map/reduce_scatter | solution.py:97
  380.1 1.3 all_to_all.21
  381.4 8.5 all-to-all-start.1
  389.9 0.0 all-reduce.6.cloned.1.call-start
  389.9 1.3 dynamic-slice
  391.8 7.0 all-to-all-done.1
  398.8 0.1 reshape.94
  398.9 1099.6 %all-gather.4.cloned.1.call-done = bf16[512,2,2048]{2,1,0:T(2,128)(2,1)} async-done(((bf16[1,2,2048]{2,1,0:T(2,128)(2,1)}), bf16[512,2,2048]{2,1,0:T(2,128)(2,1)}) %all-gather.4.cloned.1.call-update) | async-done | bytes 4194320 | tf_op jit(solution)/shard_map/all_gather | solution.py:54
  1498.5 7.2 reshape.98
  1505.7 1.1 constant_dynamic-slice_fusion.1
  1506.8 0.3 copy.42
  1507.0 5.0 fusion.38
  1512.0 0.2 copy.50
  1512.2 0.9 convert_element_type.68
  1513.1 0.0 all-reduce.6.cloned.1.call-update
  1513.2 0.2 all-reduce.4.cloned.1.call-start
  1513.4 1.3 fusion
  1514.7 1.6 copy.46
  1516.3 0.0 copy-start.1
  1516.3 1.9 copy-done.1
  1518.3 2.0 fusion.1
  1520.3 0.0 copy-done.3
  1520.3 0.0 copy-done.6
  1520.3 5.0 fusion.14
  1525.3 0.0 all-reduce.4.cloned.1.call-update
  1525.3 91.5 %all-reduce.6.cloned.1.call-done = bf16[16,2048]{1,0:T(8,128)(2,1)} async-done(((bf16[16,2048]{1,0:T(8,128)(2,1)}), bf16[16,2048]{1,0:T(8,128)(2,1)}) %all-reduce.6.cloned.1.call-update) | async-done | bytes 65552
  1616.8 0.8 constant_dynamic-slice_fusion
  1617.6 0.1 reshape.93
  1617.7 0.1 fusion.57
  1617.8 0.3 fusion.56
  1618.1 0.0 copy-done.2
  1618.1 0.2 fusion.51
  1618.3 0.1 div.41
  1618.4 0.8 fusion.54
  1619.2 272.9 %all-reduce.4.cloned.1.call-done = f32[1024,128]{1,0:T(8,128)} async-done(((f32[1024,128]{1,0:T(8,128)}), f32[1024,128]{1,0:T(8,128)}) %all-reduce.4.cloned.1.call-update) | async-done | bytes 524304 | tf_op jit(solution)/shard_map/psum | solution.py:99
  1892.0 1.9 broadcast_multiply_fusion
  (9 shorter events, 0.0 us)
Async XLA Ops:
  8.0 3.0 copy-start
  8.0 372.1 %reduce-scatter.2.cloned.1.call-start = ((), (), s32[]{:S(2)}) async-start(), calls=%async_computation.3 | async-start | bytes 1064960 | tf_op jit(solution)/shard_map/reduce_scatter | solution.py:97
  21.7 5.6 copy-start.4
  75.0 22.1 %copy-start.5 = (bf16[256,32]{0,1:T(8,128)(2,1)S(1)}, bf16[256,32]{0,1:T(8,128)(2,1)}, u32[]{:S(2)}) copy-start(bf16[256,32]{0,1:T(8,128)(2,1)} %param.8) | copy-start | bytes 49156
  97.0 1401.5 %all-gather.4.cloned.1.call-start = ((), (), s32[]{:S(2)}) async-start(), calls=%async_computation.5 | async-start | bytes 4202496 | tf_op jit(solution)/shard_map/all_gather | solution.py:54
  381.4 17.4 all-to-all-start.1
  389.9 1227.0 %all-reduce.6.cloned.1.call-start = ((), (), s32[]{:S(2)}) async-start(), calls=%async_computation.6 | async-start | bytes 131072
  1513.2 378.9 %all-reduce.4.cloned.1.call-start = ((), (), s32[]{:S(2)}) async-start(), calls=%async_computation.4 | async-start | bytes 1048576 | tf_op jit(solution)/shard_map/psum | solution.py:99
  1516.3 1.9 copy-start.1
  1518.3 2.1 copy-start.3
  1518.3 2.1 copy-start.6
  1520.3 97.8 %copy-start.2 = (bf16[2,64,256]{2,1,0:T(8,128)(2,1)S(1)}, bf16[2,64,256]{2,1,0:T(8,128)(2,1)}, u32[]{:S(2)}) copy-start(bf16[2,64,256]{2,1,0:T(8,128)(2,1)} %param.6) | copy-start | bytes 196612
Sparse Core Ops, SparseCore 0:
  97.1 282.9 reduce-scatter.1
Sparse Core Ops, SparseCore 1:
  100.3 1398.1 all-gather.3
  1513.2 103.5 all-reduce.5
  1622.3 269.7 all-reduce.3
where the time goes:
time: 1900 us
  waiting for transfers between devices  1750 us (92%)
  blocking collectives  62.4 us (3%)
  local copies, waits for them, and re-layouts  31.9 us (2%)
  matrix products  23 us (1%)
    all_gather x1, waiting for transfers between devices, on_device(): right_all = lax.all_gather(right_own, ('row', 'col'), axis=0, tiled=True)  1100 us
    reduce_scatter x1, waiting for transfers between devices, on_device(): lax.psum_scatter(spread_back, 'row', scatter_dimension=0, tiled=True)  282 us
    psum x1, waiting for transfers between devices, on_device(): weight_total = lax.psum(weight_part, ('row', 'col'))  273 us
    unnamed x5, waiting for transfers between devices  91.6 us
    all_gather x1, blocking collectives, on_device(): left_tile_block = lax.all_gather(left_own, 'col', axis=0, tiled=True)  42.2 us
  transfers between devices with their start and end apart: 5, of which 5 were waited for; matrix products, arithmetic and copies ran while one was open for 1% of the time, Pallas kernels for 0%

commit v1 on v0

v1 whole, which is shorter than its diff:
```python
import functools

import jax
import jax.numpy as jnp
from jax import lax
from jax.experimental import pallas as pl
from jax.experimental.pallas import tpu as pltpu
from jax.sharding import PartitionSpec as P

EPSILON = 1e-05
MESH = pl.DeviceIdType.MESH
BF = jnp.bfloat16
F32 = jnp.float32


def f32dot(a, b, dims):
    return lax.dot_general(a, b, (dims, ((), ())), preferred_element_type=F32)


def kernel(
    acts, w1, w2, w_hbm, bias, g_hbm,
    pair_hbm, sens, wg_out,
    scaled_v, inv_v, wcat, wbuf, wf, wc, gcat, lbuf, lm, ltc, xr, rraw, rf, r2d, rt,
    tmat, umat, grb, grx, gf, grs, gry, grz, gro, gls, glr,
    wg32, wgb, wgx, whb, wy, wzb, wxb, wfin, pbuf,
    s_loc, s_g, s_p, l_s, l_r, a_s, a_r, b_s, b_r, c_s, c_r, x_s, x_r, y_s, y_r, o_s, o_r, gl_s, gl_r,
    w0_s, w0_r, w1_s, w1_r, w2_s, w2_r, w3_s, w3_r, w4_s, w4_r, w5_s, w5_r,
):
    row = lax.axis_index("row")
    col = lax.axis_index("col")
    zl, y, k = row // 16, (row // 2) % 8, row % 2
    zh, x = col // 4, col % 4
    z = zh * 4 + zl
    other = 1 - k
    cy = (2 * y + 1) % 9
    home = row // 8
    fy = (5 * col + 4) % 9
    mq = (row % 8) // 2

    def row_of(a, b, c):
        return a * 16 + b * 2 + c

    y_peers = [(row_of(zl, (y + d) % 8, k), col) for d in range(1, 8)]
    col_peers = [(row, (col + d) % 8) for d in range(1, 8)]
    x_peers = [(row, zh * 4 + (x + d) % 4) for d in range(1, 4)]
    z_peers = [
        (row_of(((z + d) % 8) % 4, y, k), (((z + d) % 8) // 4) * 4 + x) for d in range(1, 8)
    ]
    twin = (row_of(zl, y, other), col)
    takers = [(row_of(a, fy, k), home) for a in range(4)]
    owners = [(8 * col + 2 * m + k, cy) for m in range(4)]

    def send(src, dst, ss, rs, dev):
        cp = pltpu.make_async_remote_copy(
            src_ref=src, dst_ref=dst, send_sem=ss, recv_sem=rs, device_id=dev, device_id_type=MESH
        )
        cp.start()
        return cp

    loads = [pltpu.make_async_copy(w_hbm, wbuf, s_loc.at[0])]
    loads[0].start()
    gloads = []
    for i in range(16):
        cp = pltpu.make_async_copy(g_hbm.at[i], gcat.at[:, pl.ds(i * 128, 128)], s_g.at[i])
        cp.start()
        gloads.append(cp)

    barrier = pltpu.get_barrier_semaphore()
    greet = y_peers + col_peers + z_peers + [twin] + takers + owners
    for dev in greet:
        pl.semaphore_signal(barrier, inc=1, device_id=dev, device_id_type=MESH)

    wcat[...] = jnp.concatenate([w1[...], w2[...], jnp.zeros((256, 64), BF)], axis=1)
    xv = acts[...].astype(F32).reshape(128, 256)
    center = jnp.mean(xv, axis=-1, keepdims=True)
    diff = xv - center
    inv = lax.rsqrt(jnp.mean(diff * diff, axis=-1, keepdims=True) + EPSILON)
    scaled = diff * inv
    scaled_v[...] = scaled
    inv_v[...] = inv
    proj = f32dot(scaled.astype(BF), wcat[...], ((1,), (0,)))
    projt = proj.T
    low = lax.broadcasted_iota(jnp.int32, (16, 128), 1) < 64
    lbuf[col] = projt[0:32].astype(BF)
    ra, rb = projt[32:48], projt[48:64]
    xr[0:16] = jnp.where(low, ra, pltpu.roll(rb, 64, 1)).astype(BF)
    xr[16:32] = jnp.where(low, pltpu.roll(ra, 64, 1), rb).astype(BF)

    pl.semaphore_wait(barrier, len(greet))

    sent = []
    l_cp = [
        send(lbuf.at[col], lbuf.at[col], l_s.at[d], l_r.at[d], col_peers[d]) for d in range(7)
    ]
    a_cp = [
        send(xr, rraw.at[mq, k, col], a_s.at[a], a_r.at[mq], takers[a]) for a in range(4)
    ]
    sent += l_cp + a_cp

    loads[0].wait()
    wf[...] = wbuf[...].astype(F32)
    for e in range(32):
        pos = (e % 16) * 2 + e // 16
        wc[:, pos * 128:(pos + 1) * 128] = wf[pl.ds(e, 32, stride=32), :].astype(BF)

    for cp in l_cp:
        cp.wait_recv()
    for c in range(8):
        blk = lbuf[c]
        ltc[:, c * 128:(c + 1) * 128] = blk
        lm[c * 128:(c + 1) * 128, :] = blk.astype(F32).T.astype(BF)

    for m in range(4):
        pltpu.make_async_remote_copy(
            src_ref=xr, dst_ref=rraw.at[m, k, cy], send_sem=a_s.at[m], recv_sem=a_r.at[m],
            device_id=twin, device_id_type=MESH,
        ).wait_recv()
    b_cp = [
        send(rraw.at[:, k, cy], rraw.at[:, k, cy], b_s.at[d], b_r.at[d], y_peers[d])
        for d in range(7)
    ]
    c_cp = [send(rraw.at[:, k, cy], rraw.at[:, k, cy], c_s.at[0], c_r.at[0], twin)]
    sent += b_cp

    def t_step(n, _):
        t, ib = n // 4, n % 4
        r0 = pl.multiple_of(ib * 256, 256)
        c0 = pl.multiple_of(t * 256, 256)
        res = f32dot(lm[pl.ds(r0, 256), :], wc[:, pl.ds(c0, 256)], ((1,), (0,))) * (1.0 / 64.0)
        res = res.astype(BF)
        for i in range(4):
            for h in range(2):
                tmat[
                    pl.ds(pl.multiple_of(t * 128 + h * 64, 64), 64),
                    pl.ds(pl.multiple_of(ib * 512 + i * 128, 128), 128),
                ] = res[i * 64:(i + 1) * 64, h * 128:(h + 1) * 128]
        return 0

    lax.fori_loop(0, 64, t_step, 0)

    for cp in gloads:
        cp.wait()

    def gr_step(n, _):
        res = f32dot(gcat[...], tmat[pl.ds(pl.multiple_of(n * 256, 256), 256), :], ((1,), (1,)))
        res = res.astype(BF)
        for tt in range(2):
            for q in range(8):
                grb[q % 2, n * 2 + tt, (q // 2) * 16:(q // 2 + 1) * 16, :] = res[
                    q * 16:(q + 1) * 16, tt * 128:(tt + 1) * 128
                ]
        return 0

    lax.fori_loop(0, 8, gr_step, 0)
    x_cp = send(grb.at[other], grx, x_s, x_r, twin)
    sent.append(x_cp)

    for d in range(7):
        b_cp[d].wait_recv()
        cs = (2 * ((y + 7 - d) % 8) + 1) % 9
        c_cp.append(
            send(rraw.at[:, k, cs], rraw.at[:, k, cs], c_s.at[d + 1], c_r.at[d + 1], twin)
        )
    sent += c_cp

    x_cp.wait_recv()

    def gs_step(t, _):
        gf[pl.ds(t, 64, stride=16), :] = grb[k, t].astype(F32) + grx[t].astype(F32)
        return 0

    lax.fori_loop(0, 16, gs_step, 0)

    def gp_step(m, _):
        blk = gf[pl.ds(pl.multiple_of(m * 256, 256), 256), :].astype(BF)
        grs[m] = blk.reshape(8, 32, 128)
        return 0

    lax.fori_loop(0, 4, gp_step, 0)
    y_cp = []
    for d in range(7):
        cs = (2 * ((y + d + 1) % 8) + 1) % 9
        y_cp.append(send(grs.at[:, cs], gry.at[d], y_s.at[d], y_r.at[d], y_peers[d]))
    sent += y_cp

    for cp in c_cp:
        cp.wait_recv()

    def rf_step(n, _):
        blk = rraw[n // 2, n % 2].reshape(256, 128)
        rf[pl.ds(pl.multiple_of(n * 256, 256), 256), :] = blk.astype(F32)
        return 0

    lax.fori_loop(0, 8, rf_step, 0)

    def rt_step(t, _):
        blk = rf[pl.ds(t, 128, stride=16), :]
        t0 = pl.multiple_of(t * 128, 128)
        r2d[:, pl.ds(t0, 128)] = blk.astype(BF)
        rt[pl.ds(t0, 128), :] = blk.T.astype(BF)
        return 0

    lax.fori_loop(0, 16, rt_step, 0)

    def u_step(t, _):
        t0 = pl.multiple_of(t * 128, 128)
        lhs = rt[pl.ds(t0, 128), :]
        for ib in range(4):
            res = f32dot(lhs, gcat[:, ib * 512:(ib + 1) * 512], ((1,), (0,))).astype(BF)
            for i in range(4):
                for h in range(2):
                    umat[
                        (ib * 4 + i) * 64:(ib * 4 + i + 1) * 64,
                        pl.ds(pl.multiple_of(t * 256 + h * 128, 128), 128),
                    ] = res[h * 64:(h + 1) * 64, i * 128:(i + 1) * 128]
        wt = f32dot(ltc[...], umat[:, pl.ds(pl.multiple_of(t * 256, 256), 256)], ((1,), (0,)))
        for h in range(2):
            part = wt[:, h * 128:(h + 1) * 128]
            r0 = pl.multiple_of(t * 32, 32)
            wg32[h, pl.ds(r0, 32), :] = part
            wgb[h, pl.ds(r0, 32), :] = part.astype(BF)
        return 0

    lax.fori_loop(0, 16, u_step, 0)

    w0_cp = send(wgb.at[other], wgx, w0_s, w0_r, twin)
    sent.append(w0_cp)
    w0_cp.wait_recv()
    for n in range(8):
        whb[n] = (
            wg32[k, n * 64:(n + 1) * 64, :] + wgx[n * 64:(n + 1) * 64, :].astype(F32)
        ).astype(BF)
    w1_cp = [
        send(whb.at[(y + d + 1) % 8], wy.at[d], w1_s.at[d], w1_r.at[d], y_peers[d])
        for d in range(7)
    ]
    sent += w1_cp

    def gl_step(n, _):
        res = f32dot(wc[...], umat[pl.ds(pl.multiple_of(n * 256, 256), 256), :], ((1,), (1,)))
        res = (res * (1.0 / 64.0)).astype(BF)
        gls[n * 2] = res[:, 0:128]
        gls[n * 2 + 1] = res[:, 128:256]
        return 0

    lax.fori_loop(0, 4, gl_step, 0)
    gl_cp = [
        send(gls.at[(col + d + 1) % 8], glr.at[d], gl_s.at[d], gl_r.at[d], col_peers[d])
        for d in range(7)
    ]
    sent += gl_cp

    for cp in y_cp:
        cp.wait_recv()
    for m in range(4):
        acc = grs[m, cy].astype(F32)
        for d in range(7):
            acc = acc + gry[d, m].astype(F32)
        grz[m] = acc.astype(BF)
    o_cp = [send(grz.at[m], gro.at[zl], o_s.at[m], o_r.at[zl], owners[m]) for m in range(4)]
    sent += o_cp

    for cp in w1_cp:
        cp.wait_recv()
    acc = whb[y].astype(F32)
    for d in range(7):
        acc = acc + wy[d].astype(F32)
    wzb[z] = acc.astype(BF)
    w2_cp = [
        send(wzb.at[z], wzb.at[z], w2_s.at[d], w2_r.at[d], z_peers[d]) for d in range(7)
    ]
    sent += w2_cp

    def pair_step(n, _):
        c0 = pl.multiple_of(n * 256, 256)
        res = f32dot(r2d[...], tmat[:, pl.ds(c0, 256)], ((1,), (0,)))
        for i in range(2):
            pbuf[n * 2 + i] = (res[:, i * 128:(i + 1) * 128] + bias[...]).astype(BF)
        return 0

    lax.fori_loop(0, 8, pair_step, 0)
    p_cp = pltpu.make_async_copy(pbuf, pair_hbm, s_p)
    p_cp.start()

    for cp in w2_cp:
        cp.wait_recv()
    acc = wzb[0].astype(F32)
    for n in range(1, 8):
        acc = acc + wzb[n].astype(F32)
    wxb[x] = acc.astype(BF)
    w3_cp = [
        send(wxb.at[x], wxb.at[x], w3_s.at[d], w3_r.at[d], x_peers[d]) for d in range(3)
    ]
    sent += w3_cp
    for cp in w3_cp:
        cp.wait_recv()
    acc = wxb[0].astype(F32)
    for n in range(1, 4):
        acc = acc + wxb[n].astype(F32)
    wfin[k, y] = acc.astype(BF)
    w4_cp = [
        send(wfin.at[k, y], wfin.at[k, y], w4_s.at[d], w4_r.at[d], y_peers[d]) for d in range(7)
    ]
    w5_cp = [send(wfin.at[k, y], wfin.at[k, y], w5_s.at[0], w5_r.at[0], twin)]
    sent += w4_cp

    for cp in gl_cp:
        cp.wait_recv()
    gl = gls[col].astype(F32)
    for d in range(7):
        gl = gl + glr[d].astype(F32)
    for m in range(4):
        pltpu.make_async_remote_copy(
            src_ref=grz.at[m], dst_ref=gro.at[m], send_sem=o_s.at[m], recv_sem=o_r.at[m],
            device_id=twin, device_id_type=MESH,
        ).wait_recv()
    gr = gro[0].astype(F32)
    for m in range(1, 4):
        gr = gr + gro[m].astype(F32)
    x0, x1 = gr[0:16], gr[16:32]
    ga = jnp.where(low, x0, pltpu.roll(x1, 64, 1))
    gb = jnp.where(low, pltpu.roll(x0, 64, 1), x1)
    gt = jnp.concatenate([gl, ga, gb, jnp.zeros((64, 128), F32)], axis=0).T
    hi = gt.astype(BF)
    rest = gt - hi.astype(F32)
    mid = rest.astype(BF)
    lo = (rest - mid.astype(F32)).astype(BF)
    wv = wcat[...]
    nt = ((1,), (1,))
    gn = f32dot(hi, wv, nt) + (f32dot(mid, wv, nt) + f32dot(lo, wv, nt))
    sc = scaled_v[...]
    mean_grad = jnp.mean(gn, axis=-1, keepdims=True)
    mean_cross = jnp.mean(gn * sc, axis=-1, keepdims=True)
    res = inv_v[...] * (gn - mean_grad - sc * mean_cross)
    sens[...] = res.astype(BF).reshape(2, 64, 256)

    for d in range(7):
        w4_cp[d].wait_recv()
        ys = (y + 7 - d) % 8
        w5_cp.append(
            send(wfin.at[k, ys], wfin.at[k, ys], w5_s.at[d + 1], w5_r.at[d + 1], twin)
        )
    sent += w5_cp
    for cp in w5_cp:
        cp.wait_recv()
    for h in range(2):
        for n in range(8):
            blk = wfin[h, n].astype(F32) * (8.0 / 65536.0)
            for tt in range(2):
                e = h * 16 + n * 2 + tt
                wg_out[pl.ds(e, 32, stride=32), :] = blk[tt * 32:(tt + 1) * 32]
    p_cp.wait()
    for cp in sent:
        cp.wait_send()


def on_device(acts, w1, w2, w, bias, g):
    vm = pl.BlockSpec(memory_space=pltpu.VMEM)
    anys = pl.BlockSpec(memory_space=pl.ANY)
    dma = pltpu.SemaphoreType.DMA
    scratch = [
        ((128, 256), F32), ((128, 1), F32), ((256, 128), BF), ((1024, 128), BF), ((1024, 128), F32),
        ((32, 4096), BF), ((128, 2048), BF), ((8, 32, 128), BF), ((1024, 32), BF), ((32, 1024), BF),
        ((32, 128), BF), ((4, 2, 8, 32, 128), BF), ((2048, 128), F32), ((128, 2048), BF),
        ((2048, 128), BF),
        ((2048, 2048), BF), ((1024, 4096), BF), ((2, 16, 64, 128), BF), ((16, 64, 128), BF),
        ((1024, 128), F32), ((4, 8, 32, 128), BF), ((7, 4, 32, 128), BF), ((4, 32, 128), BF),
        ((4, 32, 128), BF), ((8, 32, 128), BF), ((7, 32, 128), BF),
        ((2, 512, 128), F32), ((2, 512, 128), BF), ((512, 128), BF), ((8, 64, 128), BF),
        ((7, 64, 128), BF), ((8, 64, 128), BF), ((4, 64, 128), BF), ((2, 8, 64, 128), BF),
        ((16, 128, 128), BF),
    ]
    scratch = [pltpu.VMEM(s, d) for s, d in scratch]
    scratch += [dma((1,)), dma((16,)), dma]
    for n in (7, 4, 7, 8, 0, 7, 4, 7, 0, 7, 7, 3, 7, 8):
        scratch += [dma((n,)), dma((n,))] if n else [dma, dma]
    return pl.pallas_call(
        kernel,
        out_shape=(
            jax.ShapeDtypeStruct((16, 128, 128), BF),
            jax.ShapeDtypeStruct((2, 64, 256), BF),
            jax.ShapeDtypeStruct((1024, 128), F32),
        ),
        in_specs=[vm, vm, vm, anys, vm, anys],
        out_specs=(anys, vm, vm),
        scratch_shapes=scratch,
        compiler_params=pltpu.CompilerParams(
            collective_id=0, has_side_effects=True, vmem_limit_bytes=48 * 2**20
        ),
    )(acts, w1, w2, w, bias.reshape(1, 128), g)


def solution(mesh):
    return jax.shard_map(
        on_device,
        mesh=mesh,
        in_specs=(P(("row", "col"), None, None), P(), P(), P(), P(), P("row", "col", None)),
        out_specs=(P("row", "col", None), P(("row", "col"), None, None), P()),
        check_vma=False,
    )
```

time: 1900 us -> 88.6 us (0.05)
  waiting for transfers between devices: 1750 us -> 0 us
  Pallas kernels: 0 us -> 81.9 us
  blocking collectives: 62.4 us -> 0 us
  local copies, waits for them, and re-layouts: 31.9 us -> 5.73 us
  matrix products: 23 us -> 0 us
    all_gather x1 -> x0, waiting for transfers between devices: 1100 us -> none  [on_device(): right_all = lax.all_gather(right_own, ('row', 'col'), axis=0, tiled=True)]
    reduce_scatter x1 -> x0, waiting for transfers between devices: 282 us -> none  [on_device(): lax.psum_scatter(spread_back, 'row', scatter_dimension=0, tiled=True)]
    psum x1 -> x0, waiting for transfers between devices: 273 us -> none  [on_device(): weight_total = lax.psum(weight_part, ('row', 'col'))]
    unnamed x5 -> x0, waiting for transfers between devices: 91.6 us -> none
    pallas_call x0 -> x1, Pallas kernels: none -> 81.9 us  [on_device(): pl.pallas_call(kernel, out_shape=(jax.ShapeDtypeStruct((16, 128, 128), BF...]
    all_gather x1 -> x0, blocking collectives: 42.2 us -> none  [on_device(): left_tile_block = lax.all_gather(left_own, 'col', axis=0, tiled=True)]
    dot_general x10 -> x0, matrix products: 23 us -> none  [the longest x1 5 us: on_device(): jnp.einsum('ijce,jse->isc', grad_outer, right_triple, preferred_element_t...]
    all_to_all x1 -> x0, blocking collectives: 20.2 us -> none  [on_device(): lax.all_to_all(right_partial.astype(jnp.bfloat16), 'col', split_axis=1, c...]
  transfers between devices with their start and end apart: 5 -> 0, of which waited for: 5 -> 0; matrix products, arithmetic and copies ran while one was open for 1% -> 0% of each run, Pallas kernels for 0% -> 0%
where the time goes in v1:
time: 88.6 us; the launch traced here: 88.3 us
  Pallas kernels  81.9 us (92%)
  local copies, waits for them, and re-layouts  5.73 us (6%)
    pallas_call x1, Pallas kernels, on_device(): pl.pallas_call(kernel, out_shape=(jax.ShapeDtypeStruct((16, 128, 128), BF...  81.9 us
    unnamed x15, local copies, waits for them, and re-layouts  5.73 us

profile of v1, /device:TPU:1, one launch (start us, length us, event | category | flops | bytes accessed | tf_op | source)
XLA Modules:
  0.0 88.3 jit_solution(15887825220245913434)
XLA Ops:
  0.6 0.0 copy-start.4
  0.6 0.0 copy-start.2
  0.7 0.9 copy.9.w1
  1.5 0.0 copy-done.4
  1.5 0.0 copy-start.3
  1.5 0.1 copy.10.w2
  1.7 0.0 copy-done.2
  1.7 0.5 copy-done.3
  2.2 0.0 copy-start
  2.2 1.0 %copy-done = bf16[16,128,128]{2,1,0:T(8,128)(2,1)S(1)} copy-done((bf16[16,128,128]{2,1,0:T(8,128)(2,1)S(1)}, bf16[16,128,128]{2,1,0:T(8,128)(2,1)}, u32[]{:S(2)}) %copy-start) | copy-done | bytes 524312
  3.2 0.0 copy-start.1
  3.2 0.9 %copy-done.1 = bf16[1024,128]{1,0:T(8,128)(2,1)S(1)} copy-done((bf16[1024,128]{1,0:T(8,128)(2,1)S(1)}, bf16[1024,128]{1,0:T(8,128)(2,1)}, u32[]{:S(2)}) %copy-start.1) | copy-done | bytes 262168
  4.2 81.9 %shard_map.85 = (bf16[16,128,128]{2,1,0:T(8,128)(2,1)S(1)}, bf16[2,64,256]{2,1,0:T(8,128)(2,1)S(1)}, f32[1024,128]{1,0:T(8,128)S(1)}) custom-call(bf16[2,64,256]{2,1,0:T(8,128)(2,1)S(1)} %copy-done.2, bf16[256,32]{1,0:T(8,128)(2,1)S(1)} %copy.9.w1, bf16[256,32]{1,0:T(8,128)(2,1)S(1)} %copy.10.w2, bf16[1024,128]{1,0:T(8,128)(2,1)S(1)} %copy-done.1, ...), custom_call_target="tpu_custom_call" | custom-call | tf_op jit(solution)/shard_map/pallas_call | solution.py:377
  86.1 0.8 copy.14
  86.9 0.6 copy.15
  87.5 0.8 copy.16
Async XLA Ops:
  0.6 0.9 %copy-start.4 = (bf16[256,32]{0,1:T(8,128)(2,1)S(1)}, bf16[256,32]{0,1:T(8,128)(2,1)}, u32[]{:S(2)}) copy-start(bf16[256,32]{0,1:T(8,128)(2,1)} %param.8) | copy-start | bytes 49156
  0.6 1.0 %copy-start.2 = (bf16[2,64,256]{2,1,0:T(8,128)(2,1)S(1)}, bf16[2,64,256]{2,1,0:T(8,128)(2,1)}, u32[]{:S(2)}) copy-start(bf16[2,64,256]{2,1,0:T(8,128)(2,1)} %acts.1) | copy-start | bytes 196612
  1.5 0.7 copy-start.3
  2.2 1.0 %copy-start = (bf16[16,128,128]{2,1,0:T(8,128)(2,1)S(1)}, bf16[16,128,128]{2,1,0:T(8,128)(2,1)}, u32[]{:S(2)}) copy-start(bf16[16,128,128]{2,1,0:T(8,128)(2,1)} %g_hbm.1) | copy-start | bytes 1572868
  3.2 0.9 %copy-start.1 = (bf16[1024,128]{1,0:T(8,128)(2,1)S(1)}, bf16[1024,128]{1,0:T(8,128)(2,1)}, u32[]{:S(2)}) copy-start(bf16[1024,128]{1,0:T(8,128)(2,1)} %w_hbm.1) | copy-start | bytes 786436

commit v2 on v1

v2 whole, which is shorter than its diff:
```python
import functools

import jax
import jax.numpy as jnp
from jax import lax
from jax.experimental import pallas as pl
from jax.experimental.pallas import tpu as pltpu
from jax.sharding import PartitionSpec as P

EPSILON = 1e-05
MESH = pl.DeviceIdType.MESH
BF = jnp.bfloat16
F32 = jnp.float32


def f32dot(a, b, dims):
    return lax.dot_general(a, b, (dims, ((), ())), preferred_element_type=F32)


def kernel(
    acts_hbm, w1_hbm, w2_hbm, w_hbm, bias_hbm, g_hbm,
    pair_hbm, sens, wg_out,
    acts, bias, scaled_v, inv_v, wcat, wbuf, wf, wc, gcat, lbuf, lm, ltc, xr, rraw, rf, r2d, rt,
    tmat, umat, grb, grx, gf, grs, gry, gry2, grz, gro, gls, glr,
    wg32, wgb, wgx, whb, wy, wzb, wxb, wfin, pbuf,
    s_loc, s_g, s_p, l_s, l_r, a_s, a_r, b_s, b_r, c_s, c_r, x_s, x_r, y_s, y_r, o_s, o_r, gl_s, gl_r,
    w0_s, w0_r, w1_s, w1_r, w2_s, w2_r, w3_s, w3_r, w4_s, w4_r, w5_s, w5_r,
):
    row = lax.axis_index("row")
    col = lax.axis_index("col")
    zl, y, k = row // 16, (row // 2) % 8, row % 2
    zh, x = col // 4, col % 4
    z = zh * 4 + zl
    other = 1 - k
    home = row // 8
    mq = y % 4
    mine = (y + 2) % 4
    y_src = 4 * (col % 2) + mine

    def at(yy, zz, xx=x, kk=k):
        return ((zz % 4) * 16 + yy * 2 + kk, (zz // 4) * 4 + xx)

    y_near = [at((y + d) % 8, z) for d in (1, 7, 2, 6)]
    col_peers = [(row, (col + d) % 8) for d in range(1, 8)]
    x_peers = [at(y, z, (x + d) % 4) for d in range(1, 4)]
    first, second = y * other + z * k, z * other + y * k
    first_peers = [at((y + d * other) % 8, (z + d * k) % 8) for d in range(1, 8)]
    second_peers = [at((y + d * k) % 8, (z + d * other) % 8) for d in range(1, 8)]
    twin = at(y, z, x, other)
    takers = [(a * 16 + ((y + d) % 8) * 2 + k, home) for d in (2, 6) for a in range(4)]
    owners = [(8 * col + 2 * mine + k, c) for c in range(8)]

    def send(src, dst, ss, rs, dev):
        cp = pltpu.make_async_remote_copy(
            src_ref=src, dst_ref=dst, send_sem=ss, recv_sem=rs, device_id=dev, device_id_type=MESH
        )
        cp.start()
        return cp

    def wait_for(dst, ss, rs):
        pltpu.make_async_remote_copy(
            src_ref=dst, dst_ref=dst, send_sem=ss, recv_sem=rs, device_id=twin, device_id_type=MESH
        ).wait_recv()

    loads = [
        pltpu.make_async_copy(src, dst, s_loc.at[n])
        for n, (src, dst) in enumerate(
            [(acts_hbm, acts), (w1_hbm, wcat.at[0:32]), (w2_hbm, wcat.at[32:64]), (w_hbm, wbuf),
             (bias_hbm, bias)]
        )
    ]
    for cp in loads:
        cp.start()

    barrier = pltpu.get_barrier_semaphore()
    greet = takers + owners + col_peers + first_peers + second_peers + y_near + [twin]
    for dev in greet:
        pl.semaphore_signal(barrier, inc=1, device_id=dev, device_id_type=MESH)

    gloads = []
    for i in range(16):
        cp = pltpu.make_async_copy(g_hbm.at[i], gcat.at[:, pl.ds(i * 128, 128)], s_g.at[i])
        cp.start()
        gloads.append(cp)
    wcat[64:128] = jnp.zeros((64, 256), BF)

    loads[0].wait()
    xv = acts[...].astype(F32).reshape(128, 256)
    center = jnp.mean(xv, axis=-1, keepdims=True)
    diff = xv - center
    inv = lax.rsqrt(jnp.mean(diff * diff, axis=-1, keepdims=True) + EPSILON)
    scaled = diff * inv
    scaled_v[...] = scaled
    inv_v[...] = inv
    loads[1].wait()
    loads[2].wait()
    projt = f32dot(wcat[0:64], scaled.astype(BF), ((1,), (1,)))
    low = lax.broadcasted_iota(jnp.int32, (16, 128), 1) < 64
    lbuf[col] = projt[0:32].astype(BF)
    ra, rb = projt[32:48], projt[48:64]
    xr[0:16] = jnp.where(low, ra, pltpu.roll(rb, 64, 1)).astype(BF)
    xr[16:32] = jnp.where(low, pltpu.roll(ra, 64, 1), rb).astype(BF)

    pl.semaphore_wait(barrier, len(greet))

    sent = []
    a_cp = [
        send(xr, rraw.at[mq, k, col], a_s.at[n], a_r.at[col], takers[n]) for n in range(8)
    ]
    l_cp = [
        send(lbuf.at[col], lbuf.at[col], l_s.at[d], l_r.at[d], col_peers[d]) for d in range(7)
    ]
    sent += l_cp + a_cp

    loads[3].wait()
    loads[4].wait()
    wf[...] = wbuf[...].astype(F32)
    for e in range(32):
        pos = (e % 16) * 2 + e // 16
        wc[:, pos * 128:(pos + 1) * 128] = (wf[pl.ds(e, 32, stride=32), :] * (1.0 / 64.0)).astype(BF)

    for cp in l_cp:
        cp.wait_recv()
    for c in range(8):
        blk = lbuf[c]
        ltc[:, c * 128:(c + 1) * 128] = blk
        lm[c * 128:(c + 1) * 128, :] = blk.astype(F32).T.astype(BF)

    for c in range(8):
        wait_for(rraw.at[mine, k, c], a_s.at[c], a_r.at[c])
    part = [(0, 8), (0, 8), (0, 4), (4, 4)]
    b_cp = []
    for n in range(4):
        piece = rraw.at[mine, k, pl.ds(part[n][0], part[n][1])]
        b_cp.append(send(piece, piece, b_s.at[n], b_r.at[n], y_near[n]))
    c_cp = [send(rraw.at[mine, k], rraw.at[mine, k], c_s.at[4], c_r.at[4], twin)]
    sent += b_cp

    def t_step(t, _):
        c0 = pl.multiple_of(t * 256, 256)
        r0 = pl.multiple_of(t * 128, 128)
        for ib in range(2):
            res = f32dot(lm[ib * 512:(ib + 1) * 512, :], wc[:, pl.ds(c0, 256)], ((1,), (0,)))
            res = res.astype(BF)
            for i in range(8):
                for h in range(2):
                    tmat[pl.ds(r0 + h * 64, 64), (ib * 8 + i) * 128:(ib * 8 + i + 1) * 128] = res[
                        i * 64:(i + 1) * 64, h * 128:(h + 1) * 128
                    ]
        return 0

    lax.fori_loop(0, 16, t_step, 0)

    for cp in gloads:
        cp.wait()

    def gr_step(n, _):
        res = f32dot(gcat[...], tmat[pl.ds(pl.multiple_of(n * 256, 256), 256), :], ((1,), (1,)))
        res = res.astype(BF)
        for tt in range(2):
            for q in range(8):
                grb[q % 2, n * 2 + tt, (q // 2) * 16:(q // 2 + 1) * 16, :] = res[
                    q * 16:(q + 1) * 16, tt * 128:(tt + 1) * 128
                ]
        return 0

    lax.fori_loop(0, 4, gr_step, 0)

    for n, off in enumerate((3, 1, 2, 2)):
        piece = rraw.at[(mine + off) % 4, k, pl.ds(part[n][0], part[n][1])]
        wait_for(piece, b_s.at[n], b_r.at[n])
        c_cp.append(send(piece, piece, c_s.at[n], c_r.at[n], twin))
    sent += c_cp
    for cp in c_cp:
        cp.wait_recv()

    def rf_step(n, _):
        blk = rraw[n // 2, n % 2].reshape(256, 128)
        rf[pl.ds(pl.multiple_of(n * 256, 256), 256), :] = blk.astype(F32)
        return 0

    lax.fori_loop(0, 8, rf_step, 0)

    def rt_step(t, _):
        blk = rf[pl.ds(t, 128, stride=16), :]
        t0 = pl.multiple_of(t * 128, 128)
        r2d[:, pl.ds(t0, 128)] = blk.astype(BF)
        rt[pl.ds(t0, 128), :] = blk.T.astype(BF)
        return 0

    lax.fori_loop(0, 16, rt_step, 0)

    def u_step(t, _):
        t0 = pl.multiple_of(t * 128, 128)
        lhs = rt[pl.ds(t0, 128), :]
        for ib in range(2):
            res = f32dot(lhs, gcat[:, ib * 1024:(ib + 1) * 1024], ((1,), (0,))).astype(BF)
            for i in range(8):
                for h in range(2):
                    umat[
                        (ib * 8 + i) * 64:(ib * 8 + i + 1) * 64,
                        pl.ds(pl.multiple_of(t * 256 + h * 128, 128), 128),
                    ] = res[h * 64:(h + 1) * 64, i * 128:(i + 1) * 128]
        return 0

    lax.fori_loop(0, 16, u_step, 0)

    def w_step(n, _):
        wt = f32dot(ltc[...], umat[:, pl.ds(pl.multiple_of(n * 512, 512), 512)], ((1,), (0,)))
        for tt in range(2):
            r0 = pl.multiple_of(n * 64 + tt * 32, 32)
            for h in range(2):
                piece = wt[:, (tt * 2 + h) * 128:(tt * 2 + h + 1) * 128]
                wg32[h, pl.ds(r0, 32), :] = piece
                wgb[h, pl.ds(r0, 32), :] = piece.astype(BF)
        return 0

    lax.fori_loop(0, 8, w_step, 0)

    w0_cp = send(wgb.at[other], wgx, w0_s, w0_r, twin)
    sent.append(w0_cp)
    lax.fori_loop(4, 8, gr_step, 0)
    x_cp = send(grb.at[other], grx, x_s, x_r, twin)
    sent.append(x_cp)
    w0_cp.wait_recv()
    for n in range(8):
        whb[n] = (
            wg32[k, n * 64:(n + 1) * 64, :] + wgx[n * 64:(n + 1) * 64, :].astype(F32)
        ).astype(BF)
    w1_cp = [
        send(whb.at[(first + d + 1) % 8], wy.at[d], w1_s.at[d], w1_r.at[d], first_peers[d])
        for d in range(7)
    ]
    sent += w1_cp

    def gl_step(n, _):
        res = f32dot(wc[...], umat[pl.ds(pl.multiple_of(n * 256, 256), 256), :], ((1,), (1,)))
        res = res.astype(BF)
        gls[n * 2] = res[:, 0:128]
        gls[n * 2 + 1] = res[:, 128:256]
        return 0

    lax.fori_loop(0, 4, gl_step, 0)
    gl_cp = [
        send(gls.at[(col + d + 1) % 8], glr.at[d], gl_s.at[d], gl_r.at[d], col_peers[d])
        for d in range(7)
    ]
    sent += gl_cp

    x_cp.wait_recv()

    def gs_step(t, _):
        gf[pl.ds(t, 64, stride=16), :] = grb[k, t].astype(F32) + grx[t].astype(F32)
        return 0

    lax.fori_loop(0, 16, gs_step, 0)

    def gp_step(m, _):
        blk = gf[pl.ds(pl.multiple_of(m * 256, 256), 256), :].astype(BF)
        grs[m] = blk.reshape(8, 32, 128)
        return 0

    lax.fori_loop(0, 4, gp_step, 0)
    y_cp = []
    for n, off in enumerate((1, 3, 2, 2)):
        piece = grs.at[(mine + off) % 4, pl.ds(part[n][0], part[n][1])]
        dst = gry.at[n] if n < 2 else gry2.at[n - 2]
        y_cp.append(send(piece, dst, y_s.at[n], y_r.at[n], y_near[n]))
    sent += y_cp

    for cp in w1_cp:
        cp.wait_recv()
    acc = whb[first].astype(F32)
    for d in range(7):
        acc = acc + wy[d].astype(F32)
    wzb[second] = acc.astype(BF)
    w2_cp = [
        send(wzb.at[second], wzb.at[second], w2_s.at[d], w2_r.at[d], second_peers[d]) for d in range(7)
    ]
    sent += w2_cp

    def pair_step(n, _):
        c0 = pl.multiple_of(n * 256, 256)
        res = f32dot(r2d[...], tmat[:, pl.ds(c0, 256)], ((1,), (0,)))
        for i in range(2):
            pbuf[n * 2 + i] = (res[:, i * 128:(i + 1) * 128] + bias[...]).astype(BF)
        return 0

    lax.fori_loop(0, 8, pair_step, 0)
    p_cp = pltpu.make_async_copy(pbuf, pair_hbm, s_p)
    p_cp.start()

    for cp in y_cp:
        cp.wait_recv()
    for c in range(8):
        acc = grs[mine, c].astype(F32) + gry[0, c].astype(F32) + gry[1, c].astype(F32)
        grz[c] = (acc + gry2[c // 4, c % 4].astype(F32)).astype(BF)
    slot = zl * 2 + ((y - y_src + 8) % 8) // 4
    o_cp = [send(grz.at[c], gro.at[slot], o_s.at[c], o_r.at[slot], owners[c]) for c in range(8)]
    sent += o_cp

    for cp in w2_cp:
        cp.wait_recv()
    acc = wzb[0].astype(F32)
    for n in range(1, 8):
        acc = acc + wzb[n].astype(F32)
    wxb[x] = acc.astype(BF)
    w3_cp = [
        send(wxb.at[x], wxb.at[x], w3_s.at[d], w3_r.at[d], x_peers[d]) for d in range(3)
    ]
    sent += w3_cp
    for cp in w3_cp:
        cp.wait_recv()
    acc = wxb[0].astype(F32)
    for n in range(1, 4):
        acc = acc + wxb[n].astype(F32)
    wfin[k, first] = acc.astype(BF)
    w4_cp = [
        send(wfin.at[k, first], wfin.at[k, first], w4_s.at[d], w4_r.at[d], first_peers[d])
        for d in range(7)
    ]
    w5_cp = [send(wfin.at[k, first], wfin.at[k, first], w5_s.at[0], w5_r.at[0], twin)]
    sent += w4_cp

    for cp in gl_cp:
        cp.wait_recv()
    gl = gls[col].astype(F32)
    for d in range(7):
        gl = gl + glr[d].astype(F32)
    for n in range(8):
        wait_for(gro.at[n], o_s.at[n], o_r.at[n])
    gr = gro[0].astype(F32)
    for n in range(1, 8):
        gr = gr + gro[n].astype(F32)
    x0, x1 = gr[0:16], gr[16:32]
    ga = jnp.where(low, x0, pltpu.roll(x1, 64, 1))
    gb = jnp.where(low, pltpu.roll(x0, 64, 1), x1)
    gt = jnp.concatenate([gl, ga, gb, jnp.zeros((64, 128), F32)], axis=0).T
    hi = gt.astype(BF)
    rest = gt - hi.astype(F32)
    mid = rest.astype(BF)
    lo = (rest - mid.astype(F32)).astype(BF)
    wv = wcat[...]
    nt = ((1,), (0,))
    gn = f32dot(hi, wv, nt) + (f32dot(mid, wv, nt) + f32dot(lo, wv, nt))
    sc = scaled_v[...]
    mean_grad = jnp.mean(gn, axis=-1, keepdims=True)
    mean_cross = jnp.mean(gn * sc, axis=-1, keepdims=True)
    res = inv_v[...] * (gn - mean_grad - sc * mean_cross)
    sens[...] = res.astype(BF).reshape(2, 64, 256)

    for d in range(7):
        w4_cp[d].wait_recv()
        ys = (first + 7 - d) % 8
        w5_cp.append(
            send(wfin.at[k, ys], wfin.at[k, ys], w5_s.at[d + 1], w5_r.at[d + 1], twin)
        )
    sent += w5_cp
    for cp in w5_cp:
        cp.wait_recv()
    for h in range(2):
        for n in range(8):
            blk = wfin[h, n].astype(F32) * (8.0 / 65536.0)
            for tt in range(2):
                e = h * 16 + n * 2 + tt
                wg_out[pl.ds(e, 32, stride=32), :] = blk[tt * 32:(tt + 1) * 32]
    p_cp.wait()
    for cp in sent:
        cp.wait_send()


def on_device(acts, w1, w2, w, bias, g):
    vm = pl.BlockSpec(memory_space=pltpu.VMEM)
    anys = pl.BlockSpec(memory_space=pl.ANY)
    dma = pltpu.SemaphoreType.DMA
    scratch = [
        ((2, 64, 256), BF), ((1, 128), F32),
        ((128, 256), F32), ((128, 1), F32), ((128, 256), BF), ((1024, 128), BF), ((1024, 128), F32),
        ((32, 4096), BF), ((128, 2048), BF), ((8, 32, 128), BF), ((1024, 32), BF), ((32, 1024), BF),
        ((32, 128), BF), ((4, 2, 8, 32, 128), BF), ((2048, 128), F32), ((128, 2048), BF),
        ((2048, 128), BF),
        ((2048, 2048), BF), ((1024, 4096), BF), ((2, 16, 64, 128), BF), ((16, 64, 128), BF),
        ((1024, 128), F32), ((4, 8, 32, 128), BF), ((2, 8, 32, 128), BF), ((2, 4, 32, 128), BF),
        ((8, 32, 128), BF), ((8, 32, 128), BF), ((8, 32, 128), BF), ((7, 32, 128), BF),
        ((2, 512, 128), F32), ((2, 512, 128), BF), ((512, 128), BF), ((8, 64, 128), BF),
        ((7, 64, 128), BF), ((8, 64, 128), BF), ((4, 64, 128), BF), ((2, 8, 64, 128), BF),
        ((16, 128, 128), BF),
    ]
    scratch = [pltpu.VMEM(s, d) for s, d in scratch]
    scratch += [dma((5,)), dma((16,)), dma]
    for n in (7, 8, 4, 5, 0, 4, 8, 7, 0, 7, 7, 3, 7, 8):
        scratch += [dma((n,)), dma((n,))] if n else [dma, dma]
    return pl.pallas_call(
        kernel,
        out_shape=(
            jax.ShapeDtypeStruct((16, 128, 128), BF),
            jax.ShapeDtypeStruct((2, 64, 256), BF),
            jax.ShapeDtypeStruct((1024, 128), F32),
        ),
        in_specs=[anys] * 6,
        out_specs=(anys, vm, vm),
        scratch_shapes=scratch,
        compiler_params=pltpu.CompilerParams(
            collective_id=0, has_side_effects=True, vmem_limit_bytes=64 * 2**20 - 65536
        ),
    )(acts, w1.T, w2.T, w, bias.reshape(1, 128), g)


def solution(mesh):
    return jax.shard_map(
        on_device,
        mesh=mesh,
        in_specs=(P(("row", "col"), None, None), P(), P(), P(), P(), P("row", "col", None)),
        out_specs=(P("row", "col", None), P(("row", "col"), None, None), P()),
        check_vma=False,
    )
```

time: 88.6 us -> 72.1 us (0.81)
  Pallas kernels: 81.9 us -> 68 us
  local copies, waits for them, and re-layouts: 5.73 us -> 3.38 us
    pallas_call x1, Pallas kernels: 81.9 us -> 68 us  [on_device(): pl.pallas_call(kernel, out_shape=(jax.ShapeDtypeStruct((16, 128, 128), BF...]
    unnamed x15 -> x7, local copies, waits for them, and re-layouts: 5.73 us -> 3.38 us
where the time goes in v2:
time: 72.1 us; the launch traced here: 72 us
  Pallas kernels  68 us (94%)
  local copies, waits for them, and re-layouts  3.38 us (5%)
    pallas_call x1, Pallas kernels, on_device(): pl.pallas_call(kernel, out_shape=(jax.ShapeDtypeStruct((16, 128, 128), BF...  68 us
    unnamed x7, local copies, waits for them, and re-layouts  3.38 us

profile of v2, /device:TPU:1, one launch (start us, length us, event | category | flops | bytes accessed | tf_op | source)
XLA Modules:
  0.0 72.0 jit_solution(11712142995099527279)
XLA Ops:
  0.6 68.0 %shard_map.85 = (bf16[16,128,128]{2,1,0:T(8,128)(2,1)}, bf16[2,64,256]{2,1,0:T(8,128)(2,1)}, f32[1024,128]{1,0:T(8,128)}) custom-call(bf16[2,64,256]{2,1,0:T(8,128)(2,1)} %acts_hbm.1, bf16[32,256]{1,0:T(8,128)(2,1)} %bitcast.3, bf16[32,256]{1,0:T(8,128)(2,1)} %bitcast.4, bf16[1024,128]{1,0:T(8,128)(2,1)} %w_hbm.1, f32[1,128]{1,0:T(1,128)} %bitcast.5, ...), custom_call_target="tpu_custom_call" | custom-call | tf_op jit(solution)/shard_map/pallas_call | solution.py:393
  68.6 0.0 copy-start.1
  68.6 0.0 copy-start
  68.6 1.9 %copy.12 = bf16[16,128,128]{2,1,0:T(8,128)(2,1)} copy(bf16[16,128,128]{2,1,0:T(8,128)(2,1)} %get-tuple-element.6) | data formatting | bytes 1048576
  70.6 0.0 copy-done.1
  70.6 0.6 copy.13
  71.2 0.0 copy-done
  71.2 0.8 %copy.14 = f32[1024,128]{1,0:T(8,128)} copy(f32[1024,128]{1,0:T(8,128)S(1)} %copy-done) | data formatting | bytes 1048576
Async XLA Ops:
  68.6 2.0 %copy-start.1 = (bf16[2,64,256]{2,1,0:T(8,128)(2,1)S(1)}, bf16[2,64,256]{2,1,0:T(8,128)(2,1)}, u32[]{:S(2)}) copy-start(bf16[2,64,256]{2,1,0:T(8,128)(2,1)} %get-tuple-element.7) | copy-start | bytes 196612
  68.6 2.6 %copy-start = (f32[1024,128]{1,0:T(8,128)S(1)}, f32[1024,128]{1,0:T(8,128)}, u32[]{:S(2)}) copy-start(f32[1024,128]{1,0:T(8,128)} %get-tuple-element.8) | copy-start | bytes 1572868

commit v3 on v2

v3 whole, which is shorter than its diff:
```python
import functools

import jax
import jax.numpy as jnp
from jax import lax
from jax.experimental import pallas as pl
from jax.experimental.pallas import tpu as pltpu
from jax.sharding import PartitionSpec as P

EPSILON = 1e-05
MESH = pl.DeviceIdType.MESH
BF = jnp.bfloat16
FAR = (4, 3, 5, 2, 6, 1, 7)
F32 = jnp.float32


def f32dot(a, b, dims):
    return lax.dot_general(a, b, (dims, ((), ())), preferred_element_type=F32)


def kernel(
    acts_hbm, w1_hbm, w2_hbm, w_hbm, bias_hbm, g_hbm,
    pair_hbm, sens_hbm, wg_hbm,
    acts, bias, scaled_v, inv_v, wcat, wbuf, wf, wc, gcat, lbuf, lm, ltc, xr, rraw, rf, r2d, rt,
    tmat, umat, grb, grx, gf, grs, gry, gry2, grz, gro, gls, glr,
    wg32, wgb, wgx, whb, wy, wzb, wxb, wfin, pbuf, sens, wg_out,
    s_loc, s_g, s_out, l_s, l_r, a_s, a_r, b_s, b_r, c_s, c_r, x_s, x_r, y_s, y_r, o_s, o_r, gl_s, gl_r,
    w0_s, w0_r, w1_s, w1_r, w2_s, w2_r, w3_s, w3_r, w4_s, w4_r, w5_s, w5_r,
):
    row = lax.axis_index("row")
    col = lax.axis_index("col")
    zl, y, k = row // 16, (row // 2) % 8, row % 2
    zh, x = col // 4, col % 4
    z = zh * 4 + zl
    other = 1 - k
    home = row // 8
    mq = y % 4
    mine = (y + 2) % 4
    y_src = 4 * (col % 2) + mine

    def at(yy, zz, xx=x, kk=k):
        return ((zz % 4) * 16 + yy * 2 + kk, (zz // 4) * 4 + xx)

    y_near = [at((y + d) % 8, z) for d in (2, 6, 1, 7)]
    col_peers = [(row, (col + d) % 8) for d in FAR]
    x_peers = [at(y, z, (x + d) % 4) for d in range(1, 4)]
    first, second = y * other + z * k, z * other + y * k
    first_peers = [at((y + d * other) % 8, (z + d * k) % 8) for d in FAR]
    second_peers = [at((y + d * k) % 8, (z + d * other) % 8) for d in FAR]
    twin = at(y, z, x, other)
    takers = [(a * 16 + ((y + d) % 8) * 2 + k, home) for d in (2, 6) for a in range(4)]
    owners = [(8 * col + 2 * mine + k, c) for c in range(8)]

    def send(src, dst, ss, rs, dev):
        cp = pltpu.make_async_remote_copy(
            src_ref=src, dst_ref=dst, send_sem=ss, recv_sem=rs, device_id=dev, device_id_type=MESH
        )
        cp.start()
        return cp

    def wait_for(dst, ss, rs):
        pltpu.make_async_remote_copy(
            src_ref=dst, dst_ref=dst, send_sem=ss, recv_sem=rs, device_id=twin, device_id_type=MESH
        ).wait_recv()

    loads = [
        pltpu.make_async_copy(src, dst, s_loc.at[n])
        for n, (src, dst) in enumerate(
            [(acts_hbm, acts), (w1_hbm, wcat.at[0:32]), (w2_hbm, wcat.at[32:64]), (w_hbm, wbuf),
             (bias_hbm, bias)]
        )
    ]
    for cp in loads:
        cp.start()

    barrier = pltpu.get_barrier_semaphore()
    greet = takers + owners + col_peers + [at((y + d) % 8, z) for d in FAR]
    greet += [at(y, (z + d) % 8) for d in FAR[1:]] + [twin]
    for dev in greet:
        pl.semaphore_signal(barrier, inc=1, device_id=dev, device_id_type=MESH)

    wcat[64:128] = jnp.zeros((64, 256), BF)

    loads[0].wait()
    xv = acts[...].astype(F32).reshape(128, 256)
    center = jnp.mean(xv, axis=-1, keepdims=True)
    diff = xv - center
    inv = lax.rsqrt(jnp.mean(diff * diff, axis=-1, keepdims=True) + EPSILON)
    scaled = diff * inv
    scaled_v[...] = scaled
    inv_v[...] = inv
    loads[1].wait()
    loads[2].wait()
    projt = f32dot(wcat[0:64], scaled.astype(BF), ((1,), (1,)))
    low = lax.broadcasted_iota(jnp.int32, (16, 128), 1) < 64
    lbuf[col] = projt[0:32].astype(BF)
    ra, rb = projt[32:48], projt[48:64]
    xr[0:16] = jnp.where(low, ra, pltpu.roll(rb, 64, 1)).astype(BF)
    xr[16:32] = jnp.where(low, pltpu.roll(ra, 64, 1), rb).astype(BF)

    pl.semaphore_wait(barrier, len(greet))

    a_cp = [
        send(xr, rraw.at[mq, k, col], a_s.at[n], a_r.at[col], takers[n]) for n in range(8)
    ]
    l_cp = [
        send(lbuf.at[col], lbuf.at[col], l_s.at[d], l_r.at[d], col_peers[d]) for d in range(7)
    ]

    gloads = []
    for i in range(16):
        cp = pltpu.make_async_copy(g_hbm.at[i], gcat.at[:, pl.ds(i * 128, 128)], s_g.at[i])
        cp.start()
        gloads.append(cp)

    loads[3].wait()
    loads[4].wait()
    wf[...] = wbuf[...].astype(F32)
    for e in range(32):
        pos = (e % 16) * 2 + e // 16
        wc[:, pos * 128:(pos + 1) * 128] = (wf[pl.ds(e, 32, stride=32), :] * (1.0 / 64.0)).astype(BF)

    for cp in l_cp:
        cp.wait_recv()
    for c in range(8):
        blk = lbuf[c]
        ltc[:, c * 128:(c + 1) * 128] = blk
        lm[c * 128:(c + 1) * 128, :] = blk.astype(F32).T.astype(BF)

    for c in range(8):
        wait_for(rraw.at[mine, k, c], a_s.at[c], a_r.at[c])
    part = [(0, 4), (4, 4), (0, 8), (0, 8)]
    b_cp = []
    for n in range(4):
        piece = rraw.at[mine, k, pl.ds(part[n][0], part[n][1])]
        b_cp.append(send(piece, piece, b_s.at[n], b_r.at[n], y_near[n]))
    c_cp = [send(rraw.at[mine, k], rraw.at[mine, k], c_s.at[4], c_r.at[4], twin)]

    def t_step(n, _):
        for ib in range(8):
            for tt in range(4):
                c0 = pl.multiple_of(n * 1024 + tt * 256, 256)
                r0 = pl.multiple_of(n * 512 + tt * 128, 128)
                res = f32dot(lm[ib * 128:(ib + 1) * 128, :], wc[:, pl.ds(c0, 256)], ((1,), (0,)))
                res = res.astype(BF)
                for i in range(2):
                    for h in range(2):
                        tmat[
                            pl.ds(r0 + h * 64, 64), (ib * 2 + i) * 128:(ib * 2 + i + 1) * 128
                        ] = res[i * 64:(i + 1) * 64, h * 128:(h + 1) * 128]
        return 0

    lax.fori_loop(0, 4, t_step, 0)

    for cp in gloads:
        cp.wait()

    def gr_step(n, _):
        res = f32dot(gcat[...], tmat[pl.ds(pl.multiple_of(n * 512, 512), 512), :], ((1,), (1,)))
        res = res.astype(BF)
        for tt in range(4):
            for q in range(8):
                grb[q % 2, n * 4 + tt, (q // 2) * 16:(q // 2 + 1) * 16, :] = res[
                    q * 16:(q + 1) * 16, tt * 128:(tt + 1) * 128
                ]
        return 0

    lax.fori_loop(0, 2, gr_step, 0)

    for n, off in ((2, 3), (3, 1), (0, 2), (1, 2)):
        piece = rraw.at[(mine + off) % 4, k, pl.ds(part[n][0], part[n][1])]
        wait_for(piece, b_s.at[n], b_r.at[n])
        c_cp.append(send(piece, piece, c_s.at[n], c_r.at[n], twin))

    def spread(kk):
        for m in range(4):
            r0 = pl.multiple_of((m * 2 + kk) * 256, 256)
            rf[pl.ds(r0, 256), :] = rraw[m, kk].reshape(256, 128).astype(F32)

    spread(k)
    for cp in c_cp:
        cp.wait_recv()
    spread(other)
    for t in range(16):
        blk = rf[pl.ds(t, 128, stride=16), :].astype(BF)
        r2d[:, t * 128:(t + 1) * 128] = blk
        rt[t * 128:(t + 1) * 128, :] = blk.T

    def u_step(n, _):
        rhs = gcat[:, pl.ds(pl.multiple_of(n * 256, 256), 256)]
        for t in range(16):
            res = f32dot(rt[t * 128:(t + 1) * 128, :], rhs, ((1,), (0,))).astype(BF)
            for i in range(2):
                for h in range(2):
                    umat[
                        pl.ds(pl.multiple_of((n * 2 + i) * 64, 64), 64),
                        t * 256 + h * 128:t * 256 + (h + 1) * 128,
                    ] = res[h * 64:(h + 1) * 64, i * 128:(i + 1) * 128]
        return 0

    lax.fori_loop(0, 8, u_step, 0)

    def w_step(n, _):
        wt = f32dot(ltc[...], umat[:, pl.ds(pl.multiple_of(n * 1024, 1024), 1024)], ((1,), (0,)))
        for tt in range(4):
            r0 = pl.multiple_of(n * 128 + tt * 32, 32)
            for h in range(2):
                piece = wt[:, (tt * 2 + h) * 128:(tt * 2 + h + 1) * 128]
                wg32[h, pl.ds(r0, 32), :] = piece
                wgb[h, pl.ds(r0, 32), :] = piece.astype(BF)
        return 0

    lax.fori_loop(0, 4, w_step, 0)

    w0_cp = send(wgb.at[other], wgx, w0_s, w0_r, twin)
    w0_cp.wait_recv()
    for n in range(8):
        whb[n] = (
            wg32[k, n * 64:(n + 1) * 64, :] + wgx[n * 64:(n + 1) * 64, :].astype(F32)
        ).astype(BF)
    w1_cp = [
        send(whb.at[(first + FAR[d]) % 8], wy.at[d], w1_s.at[d], w1_r.at[d], first_peers[d])
        for d in range(7)
    ]
    lax.fori_loop(2, 4, gr_step, 0)
    x_cp = send(grb.at[other], grx, x_s, x_r, twin)

    def gl_step(n, _):
        res = f32dot(wc[...], umat[pl.ds(pl.multiple_of(n * 512, 512), 512), :], ((1,), (1,)))
        res = res.astype(BF)
        for c in range(4):
            gls[n * 4 + c] = res[:, c * 128:(c + 1) * 128]
        return 0

    lax.fori_loop(0, 2, gl_step, 0)
    gl_cp = [
        send(gls.at[(col + FAR[d]) % 8], glr.at[d], gl_s.at[d], gl_r.at[d], col_peers[d])
        for d in range(7)
    ]

    x_cp.wait_recv()

    def gs_step(t, _):
        gf[pl.ds(t, 64, stride=16), :] = grb[k, t].astype(F32) + grx[t].astype(F32)
        return 0

    lax.fori_loop(0, 16, gs_step, 0)

    def gp_step(m, _):
        blk = gf[pl.ds(pl.multiple_of(m * 256, 256), 256), :].astype(BF)
        grs[m] = blk.reshape(8, 32, 128)
        return 0

    lax.fori_loop(0, 4, gp_step, 0)
    y_cp = []
    for n, off in enumerate((2, 2, 1, 3)):
        piece = grs.at[(mine + off) % 4, pl.ds(part[n][0], part[n][1])]
        dst = gry2.at[n] if n < 2 else gry.at[n - 2]
        y_cp.append(send(piece, dst, y_s.at[n], y_r.at[n], y_near[n]))

    for cp in l_cp + a_cp + b_cp + c_cp + [w0_cp, x_cp]:
        cp.wait_send()
    for cp in w1_cp:
        cp.wait_recv()
    acc = whb[first].astype(F32)
    for d in range(7):
        acc = acc + wy[d].astype(F32)
    wzb[second] = acc.astype(BF)
    w2_cp = [
        send(wzb.at[second], wzb.at[second], w2_s.at[d], w2_r.at[d], second_peers[d]) for d in range(7)
    ]

    def pair_step(n, _):
        c0 = pl.multiple_of(n * 512, 512)
        res = f32dot(r2d[...], tmat[:, pl.ds(c0, 512)], ((1,), (0,)))
        for i in range(4):
            pbuf[n * 4 + i] = (res[:, i * 128:(i + 1) * 128] + bias[...]).astype(BF)
        return 0

    lax.fori_loop(0, 4, pair_step, 0)
    p_cp = pltpu.make_async_copy(pbuf, pair_hbm, s_out.at[0])
    p_cp.start()

    for cp in y_cp:
        cp.wait_recv()
    for c in range(8):
        acc = grs[mine, c].astype(F32) + gry[0, c].astype(F32) + gry[1, c].astype(F32)
        grz[c] = (acc + gry2[c // 4, c % 4].astype(F32)).astype(BF)
    slot = zl * 2 + ((y - y_src + 8) % 8) // 4
    o_cp = [send(grz.at[c], gro.at[slot], o_s.at[c], o_r.at[slot], owners[c]) for c in range(8)]

    for cp in w1_cp + gl_cp + y_cp:
        cp.wait_send()
    for cp in w2_cp:
        cp.wait_recv()
    acc = wzb[0].astype(F32)
    for n in range(1, 8):
        acc = acc + wzb[n].astype(F32)
    wxb[x] = acc.astype(BF)
    w3_cp = [
        send(wxb.at[x], wxb.at[x], w3_s.at[d], w3_r.at[d], x_peers[d]) for d in range(3)
    ]
    for cp in w3_cp:
        cp.wait_recv()
    acc = wxb[0].astype(F32)
    for n in range(1, 4):
        acc = acc + wxb[n].astype(F32)
    wfin[k, first] = acc.astype(BF)
    w4_cp = [
        send(wfin.at[k, first], wfin.at[k, first], w4_s.at[d], w4_r.at[d], first_peers[d])
        for d in range(7)
    ]
    w5_cp = [send(wfin.at[k, first], wfin.at[k, first], w5_s.at[0], w5_r.at[0], twin)]

    for cp in gl_cp:
        cp.wait_recv()
    gl = gls[col].astype(F32)
    for d in range(7):
        gl = gl + glr[d].astype(F32)
    for n in range(8):
        wait_for(gro.at[n], o_s.at[n], o_r.at[n])
    gr = gro[0].astype(F32)
    for n in range(1, 8):
        gr = gr + gro[n].astype(F32)
    x0, x1 = gr[0:16], gr[16:32]
    ga = jnp.where(low, x0, pltpu.roll(x1, 64, 1))
    gb = jnp.where(low, pltpu.roll(x0, 64, 1), x1)
    gt = jnp.concatenate([gl, ga, gb, jnp.zeros((64, 128), F32)], axis=0).T
    hi = gt.astype(BF)
    rest = gt - hi.astype(F32)
    mid = rest.astype(BF)
    lo = (rest - mid.astype(F32)).astype(BF)
    wv = wcat[...]
    nt = ((1,), (0,))
    gn = f32dot(hi, wv, nt) + (f32dot(mid, wv, nt) + f32dot(lo, wv, nt))
    sc = scaled_v[...]
    mean_grad = jnp.mean(gn, axis=-1, keepdims=True)
    mean_cross = jnp.mean(gn * sc, axis=-1, keepdims=True)
    res = inv_v[...] * (gn - mean_grad - sc * mean_cross)
    sens[...] = res.astype(BF).reshape(2, 64, 256)
    s_cp = pltpu.make_async_copy(sens, sens_hbm, s_out.at[1])
    s_cp.start()
    for cp in o_cp + w2_cp + w3_cp:
        cp.wait_send()
    p_cp.wait()

    for d in range(6, -1, -1):
        w4_cp[d].wait_recv()
        ys = (first + 8 - FAR[d]) % 8
        w5_cp.append(
            send(wfin.at[k, ys], wfin.at[k, ys], w5_s.at[d + 1], w5_r.at[d + 1], twin)
        )
    for cp in w5_cp:
        cp.wait_recv()
    for h in range(2):
        for n in range(8):
            blk = wfin[h, n].astype(F32) * (8.0 / 65536.0)
            for tt in range(2):
                e = h * 16 + n * 2 + tt
                wg_out[pl.ds(e, 32, stride=32), :] = blk[tt * 32:(tt + 1) * 32]
    wg_cp = pltpu.make_async_copy(wg_out, wg_hbm, s_out.at[2])
    wg_cp.start()
    s_cp.wait()
    for cp in w4_cp + w5_cp:
        cp.wait_send()
    wg_cp.wait()


def hand_over(pair, sens, wg, pair_out, sens_out, wg_out, pair_v, sens_v, wg_v, sem_in, sem_out):
    trips = [(sens, sens_v, sens_out)]
    for n in range(2):
        part = pl.ds(n * 512, 512)
        trips.append((wg.at[part], wg_v.at[part], wg_out.at[part]))
    for n in range(2):
        part = pl.ds(n * 8, 8)
        trips.append((pair.at[part], pair_v.at[part], pair_out.at[part]))
    ins = [pltpu.make_async_copy(a, b, sem_in.at[n]) for n, (a, b, _) in enumerate(trips)]
    outs = [pltpu.make_async_copy(b, c, sem_out.at[n]) for n, (_, b, c) in enumerate(trips)]
    for cp in ins:
        cp.start()
    for a, b in zip(ins, outs):
        a.wait()
        b.start()
    for cp in outs:
        cp.wait()


def on_device(acts, w1, w2, w, bias, g):
    anys = pl.BlockSpec(memory_space=pl.ANY)
    dma = pltpu.SemaphoreType.DMA
    scratch = [
        ((2, 64, 256), BF), ((1, 128), F32),
        ((128, 256), F32), ((128, 1), F32), ((128, 256), BF), ((1024, 128), BF), ((1024, 128), F32),
        ((32, 4096), BF), ((128, 2048), BF), ((8, 32, 128), BF), ((1024, 32), BF), ((32, 1024), BF),
        ((32, 128), BF), ((4, 2, 8, 32, 128), BF), ((2048, 128), F32), ((128, 2048), BF),
        ((2048, 128), BF),
        ((2048, 2048), BF), ((1024, 4096), BF), ((2, 16, 64, 128), BF), ((16, 64, 128), BF),
        ((1024, 128), F32), ((4, 8, 32, 128), BF), ((2, 8, 32, 128), BF), ((2, 4, 32, 128), BF),
        ((8, 32, 128), BF), ((8, 32, 128), BF), ((8, 32, 128), BF), ((7, 32, 128), BF),
        ((2, 512, 128), F32), ((2, 512, 128), BF), ((512, 128), BF), ((8, 64, 128), BF),
        ((7, 64, 128), BF), ((8, 64, 128), BF), ((4, 64, 128), BF), ((2, 8, 64, 128), BF),
        ((16, 128, 128), BF), ((2, 64, 256), BF), ((1024, 128), F32),
    ]
    scratch = [pltpu.VMEM(s, d) for s, d in scratch]
    scratch += [dma((5,)), dma((16,)), dma((3,))]
    for n in (7, 8, 4, 5, 0, 4, 8, 7, 0, 7, 7, 3, 7, 8):
        scratch += [dma((n,)), dma((n,))] if n else [dma, dma]
    shapes = (
        jax.ShapeDtypeStruct((16, 128, 128), BF),
        jax.ShapeDtypeStruct((2, 64, 256), BF),
        jax.ShapeDtypeStruct((1024, 128), F32),
    )
    results = pl.pallas_call(
        kernel,
        out_shape=shapes,
        in_specs=[anys] * 6,
        out_specs=(anys,) * 3,
        scratch_shapes=scratch,
        compiler_params=pltpu.CompilerParams(
            collective_id=0, has_side_effects=True, vmem_limit_bytes=64 * 2**20 - 65536
        ),
    )(acts, w1.T, w2.T, w, bias.reshape(1, 128), g)
    return pl.pallas_call(
        hand_over,
        out_shape=shapes,
        in_specs=[anys] * 3,
        out_specs=(anys,) * 3,
        scratch_shapes=[pltpu.VMEM(o.shape, o.dtype) for o in shapes] + [dma((5,)), dma((5,))],
    )(*results)


def solution(mesh):
    return jax.shard_map(
        on_device,
        mesh=mesh,
        in_specs=(P(("row", "col"), None, None), P(), P(), P(), P(), P("row", "col", None)),
        out_specs=(P("row", "col", None), P(("row", "col"), None, None), P()),
        check_vma=False,
    )
```

time: 72.1 us -> 64.8 us (0.90)
  Pallas kernels: 68 us -> 64 us
  local copies, waits for them, and re-layouts: 3.38 us -> 0 us
    pallas_call x1 -> x2, Pallas kernels: 68 us -> 64 us  [the longest x1 61.9 us: on_device(): pl.pallas_call(kernel, out_shape=shapes, in_specs=[anys] * 6, out_specs=(...]
    unnamed x7 -> x0, local copies, waits for them, and re-layouts: 3.38 us -> none
where the time goes in v3:
time: 64.8 us; the launch traced here: 64.6 us
  Pallas kernels  64 us (99%)
    pallas_call x1, Pallas kernels, on_device(): pl.pallas_call(kernel, out_shape=shapes, in_specs=[anys] * 6, out_specs=(...  61.9 us
    pallas_call x1, Pallas kernels, on_device(): pl.pallas_call(hand_over, out_shape=shapes, in_specs=[anys] * 3, out_spec...  2.04 us

profile of v3, /device:TPU:1, one launch (start us, length us, event | category | flops | bytes accessed | tf_op | source)
XLA Modules:
  0.0 64.6 jit_solution(1515036550790641551)
XLA Ops:
  0.6 61.9 %shard_map.85 = (bf16[16,128,128]{2,1,0:T(8,128)(2,1)}, bf16[2,64,256]{2,1,0:T(8,128)(2,1)}, f32[1024,128]{1,0:T(8,128)}) custom-call(bf16[2,64,256]{2,1,0:T(8,128)(2,1)} %acts_hbm.1, bf16[32,256]{1,0:T(8,128)(2,1)} %bitcast.3, bf16[32,256]{1,0:T(8,128)(2,1)} %bitcast.4, bf16[1024,128]{1,0:T(8,128)(2,1)} %w_hbm.1, f32[1,128]{1,0:T(1,128)} %bitcast.5, ...), custom_call_target="tpu_custom_call" | custom-call | tf_op jit(solution)/shard_map/pallas_call | solution.py:413
  62.6 2.0 %shard_map.86 = (bf16[16,128,128]{2,1,0:T(8,128)(2,1)}, bf16[2,64,256]{2,1,0:T(8,128)(2,1)}, f32[1024,128]{1,0:T(8,128)}) custom-call(bf16[16,128,128]{2,1,0:T(8,128)(2,1)} %get-tuple-element.6.pair, bf16[2,64,256]{2,1,0:T(8,128)(2,1)} %get-tuple-element.7.sens, f32[1024,128]{1,0:T(8,128)} %get-tuple-element.8.wg), custom_call_target="tpu_custom_call" | custom-call | tf_op jit(solution)/shard_map/pallas_call | solution.py:423

commit v4 on v3

--- a/solution.py
+++ b/solution.py
@@ -10,7 +10,6 @@
 EPSILON = 1e-05
 MESH = pl.DeviceIdType.MESH
 BF = jnp.bfloat16
-FAR = (4, 3, 5, 2, 6, 1, 7)
 F32 = jnp.float32
 
 
@@ -18,12 +17,32 @@
     return lax.dot_general(a, b, (dims, ((), ())), preferred_element_type=F32)
 
 
+class Batch:
+    def __init__(self, count, make, start=True):
+        self.count, self.make = count, make
+        if start:
+            self.each(lambda cp: cp.start())
+
+    def each(self, act):
+        def body(n, _):
+            act(self.make(n))
+            return 0
+
+        lax.fori_loop(0, self.count, body, 0)
+
+    def wait_recv(self):
+        self.each(lambda cp: cp.wait_recv())
+
+    def wait_send(self):
+        self.each(lambda cp: cp.wait_send())
+
+
 def kernel(
     acts_hbm, w1_hbm, w2_hbm, w_hbm, bias_hbm, g_hbm,
-    pair_hbm, sens_hbm, wg_hbm,
+    pair_hbm, sens_hbm, wfin_hbm,
     acts, bias, scaled_v, inv_v, wcat, wbuf, wf, wc, gcat, lbuf, lm, ltc, xr, rraw, rf, r2d, rt,
     tmat, umat, grb, grx, gf, grs, gry, gry2, grz, gro, gls, glr,
-    wg32, wgb, wgx, whb, wy, wzb, wxb, wfin, pbuf, sens, wg_out,
+    wg32, wgb, wgx, whb, wy, wzb, wxb, wfin, pbuf, sens,
     s_loc, s_g, s_out, l_s, l_r, a_s, a_r, b_s, b_r, c_s, c_r, x_s, x_r, y_s, y_r, o_s, o_r, gl_s, gl_r,
     w0_s, w0_r, w1_s, w1_r, w2_s, w2_r, w3_s, w3_r, w4_s, w4_r, w5_s, w5_r,
 ):
@@ -42,26 +61,53 @@
         return ((zz % 4) * 16 + yy * 2 + kk, (zz // 4) * 4 + xx)
 
     y_near = [at((y + d) % 8, z) for d in (2, 6, 1, 7)]
-    col_peers = [(row, (col + d) % 8) for d in FAR]
     x_peers = [at(y, z, (x + d) % 4) for d in range(1, 4)]
     first, second = y * other + z * k, z * other + y * k
-    first_peers = [at((y + d * other) % 8, (z + d * k) % 8) for d in FAR]
-    second_peers = [at((y + d * k) % 8, (z + d * other) % 8) for d in FAR]
     twin = at(y, z, x, other)
-    takers = [(a * 16 + ((y + d) % 8) * 2 + k, home) for d in (2, 6) for a in range(4)]
-    owners = [(8 * col + 2 * mine + k, c) for c in range(8)]
-
-    def send(src, dst, ss, rs, dev):
-        cp = pltpu.make_async_remote_copy(
+
+    def link(src, dst, ss, rs, dev):
+        return pltpu.make_async_remote_copy(
             src_ref=src, dst_ref=dst, send_sem=ss, recv_sem=rs, device_id=dev, device_id_type=MESH
         )
+
+    def send(src, dst, ss, rs, dev):
+        cp = link(src, dst, ss, rs, dev)
         cp.start()
         return cp
+
+    def far(n):
+        return 4 + (1 - n % 2) * (n // 2) - (n % 2) * ((n + 1) // 2)
+
+    def first_peer(n):
+        return at((y + far(n) * other) % 8, (z + far(n) * k) % 8)
+
+    def second_peer(n):
+        return at((y + far(n) * k) % 8, (z + far(n) * other) % 8)
 
     def wait_for(dst, ss, rs):
         pltpu.make_async_remote_copy(
             src_ref=dst, dst_ref=dst, send_sem=ss, recv_sem=rs, device_id=twin, device_id_type=MESH
         ).wait_recv()
+
+    barrier = pltpu.get_barrier_semaphore()
+
+    def greet(dev):
+        pl.semaphore_signal(barrier, inc=1, device_id=dev, device_id_type=MESH)
+
+    def greet_far(n, _):
+        greet(((n % 4) * 16 + ((y + 2 + 4 * (n // 4)) % 8) * 2 + k, home))
+        greet((8 * col + 2 * mine + k, n))
+        return 0
+
+    def greet_ring(d, _):
+        greet(at((y + d) % 8, z))
+        greet(at(y, (z + d) % 8))
+        greet((row, (col + d) % 8))
+        return 0
+
+    lax.fori_loop(0, 8, greet_far, 0)
+    lax.fori_loop(1, 8, greet_ring, 0)
+    greet(twin)
 
     loads = [
         pltpu.make_async_copy(src, dst, s_loc.at[n])
@@ -72,12 +118,6 @@
     ]
     for cp in loads:
         cp.start()
-
-    barrier = pltpu.get_barrier_semaphore()
-    greet = takers + owners + col_peers + [at((y + d) % 8, z) for d in FAR]
-    greet += [at(y, (z + d) % 8) for d in FAR[1:]] + [twin]
-    for dev in greet:
-        pl.semaphore_signal(barrier, inc=1, device_id=dev, device_id_type=MESH)
 
     wcat[64:128] = jnp.zeros((64, 256), BF)
 
@@ -98,14 +138,17 @@
     xr[0:16] = jnp.where(low, ra, pltpu.roll(rb, 64, 1)).astype(BF)
     xr[16:32] = jnp.where(low, pltpu.roll(ra, 64, 1), rb).astype(BF)
 
-    pl.semaphore_wait(barrier, len(greet))
-
-    a_cp = [
-        send(xr, rraw.at[mq, k, col], a_s.at[n], a_r.at[col], takers[n]) for n in range(8)
-    ]
-    l_cp = [
-        send(lbuf.at[col], lbuf.at[col], l_s.at[d], l_r.at[d], col_peers[d]) for d in range(7)
-    ]
+    pl.semaphore_wait(barrier, 38)
+
+    def a_copy(n):
+        dev = ((n % 4) * 16 + ((y + 2 + 4 * (n // 4)) % 8) * 2 + k, home)
+        return link(xr, rraw.at[mq, k, col], a_s.at[n], a_r.at[col], dev)
+
+    def l_copy(n):
+        return link(lbuf.at[col], lbuf.at[col], l_s.at[n], l_r.at[n], (row, (col + far(n)) % 8))
+
+    a_cp = [Batch(8, a_copy)]
+    l_cp = [Batch(7, l_copy)]
 
     gloads = []
     for i in range(16):
@@ -119,13 +162,6 @@
     for e in range(32):
         pos = (e % 16) * 2 + e // 16
         wc[:, pos * 128:(pos + 1) * 128] = (wf[pl.ds(e, 32, stride=32), :] * (1.0 / 64.0)).astype(BF)
-
-    for cp in l_cp:
-        cp.wait_recv()
-    for c in range(8):
-        blk = lbuf[c]
-        ltc[:, c * 128:(c + 1) * 128] = blk
-        lm[c * 128:(c + 1) * 128, :] = blk.astype(F32).T.astype(BF)
 
     for c in range(8):
         wait_for(rraw.at[mine, k, c], a_s.at[c], a_r.at[c])
@@ -135,6 +171,13 @@
         piece = rraw.at[mine, k, pl.ds(part[n][0], part[n][1])]
         b_cp.append(send(piece, piece, b_s.at[n], b_r.at[n], y_near[n]))
     c_cp = [send(rraw.at[mine, k], rraw.at[mine, k], c_s.at[4], c_r.at[4], twin)]
+
+    for cp in l_cp:
+        cp.wait_recv()
+    for c in range(8):
+        blk = lbuf[c]
+        ltc[:, c * 128:(c + 1) * 128] = blk
+        lm[c * 128:(c + 1) * 128, :] = blk.astype(F32).T.astype(BF)
 
     def t_step(n, _):
         for ib in range(8):
@@ -200,43 +243,43 @@
 
     lax.fori_loop(0, 8, u_step, 0)
 
-    def w_step(n, _):
-        wt = f32dot(ltc[...], umat[:, pl.ds(pl.multiple_of(n * 1024, 1024), 1024)], ((1,), (0,)))
+    w0_cp = []
+    for n in range(4):
+        wt = f32dot(ltc[...], umat[:, n * 1024:(n + 1) * 1024], ((1,), (0,)))
         for tt in range(4):
-            r0 = pl.multiple_of(n * 128 + tt * 32, 32)
+            r0 = n * 128 + tt * 32
             for h in range(2):
                 piece = wt[:, (tt * 2 + h) * 128:(tt * 2 + h + 1) * 128]
-                wg32[h, pl.ds(r0, 32), :] = piece
-                wgb[h, pl.ds(r0, 32), :] = piece.astype(BF)
-        return 0
-
-    lax.fori_loop(0, 4, w_step, 0)
-
-    w0_cp = send(wgb.at[other], wgx, w0_s, w0_r, twin)
-    w0_cp.wait_recv()
-    for n in range(8):
-        whb[n] = (
-            wg32[k, n * 64:(n + 1) * 64, :] + wgx[n * 64:(n + 1) * 64, :].astype(F32)
-        ).astype(BF)
-    w1_cp = [
-        send(whb.at[(first + FAR[d]) % 8], wy.at[d], w1_s.at[d], w1_r.at[d], first_peers[d])
-        for d in range(7)
-    ]
+                wg32[h, r0:r0 + 32, :] = piece
+                wgb[h, r0:r0 + 32, :] = piece.astype(BF)
+        rows = pl.ds(n * 128, 128)
+        w0_cp.append(send(wgb.at[other, rows], wgx.at[rows], w0_s.at[n], w0_r.at[n], twin))
+    for n in range(4):
+        w0_cp[n].wait_recv()
+        for b in range(2 * n, 2 * n + 2):
+            whb[b] = (
+                wg32[k, b * 64:(b + 1) * 64, :] + wgx[b * 64:(b + 1) * 64, :].astype(F32)
+            ).astype(BF)
+    def w1_copy(n):
+        return link(
+            whb.at[(first + far(n)) % 8], wy.at[n], w1_s.at[n], w1_r.at[n], first_peer(n)
+        )
+
+    w1_cp = [Batch(7, w1_copy)]
+
     lax.fori_loop(2, 4, gr_step, 0)
     x_cp = send(grb.at[other], grx, x_s, x_r, twin)
 
-    def gl_step(n, _):
-        res = f32dot(wc[...], umat[pl.ds(pl.multiple_of(n * 512, 512), 512), :], ((1,), (1,)))
-        res = res.astype(BF)
-        for c in range(4):
-            gls[n * 4 + c] = res[:, c * 128:(c + 1) * 128]
-        return 0
-
-    lax.fori_loop(0, 2, gl_step, 0)
-    gl_cp = [
-        send(gls.at[(col + FAR[d]) % 8], glr.at[d], gl_s.at[d], gl_r.at[d], col_peers[d])
-        for d in range(7)
-    ]
+    def pair_step(n, _):
+        c0 = pl.multiple_of(n * 512, 512)
+        res = f32dot(r2d[...], tmat[:, pl.ds(c0, 512)], ((1,), (0,)))
+        for i in range(4):
+            pbuf[n * 4 + i] = (res[:, i * 128:(i + 1) * 128] + bias[...]).astype(BF)
+        return 0
+
+    lax.fori_loop(0, 4, pair_step, 0)
+    p_cp = pltpu.make_async_copy(pbuf, pair_hbm, s_out.at[0])
+    p_cp.start()
 
     x_cp.wait_recv()
 
@@ -258,7 +301,7 @@
         dst = gry2.at[n] if n < 2 else gry.at[n - 2]
         y_cp.append(send(piece, dst, y_s.at[n], y_r.at[n], y_near[n]))
 
-    for cp in l_cp + a_cp + b_cp + c_cp + [w0_cp, x_cp]:
+    for cp in l_cp + a_cp + b_cp + c_cp + w0_cp + [x_cp]:
         cp.wait_send()
     for cp in w1_cp:
         cp.wait_recv()
@@ -266,20 +309,26 @@
     for d in range(7):
         acc = acc + wy[d].astype(F32)
     wzb[second] = acc.astype(BF)
-    w2_cp = [
-        send(wzb.at[second], wzb.at[second], w2_s.at[d], w2_r.at[d], second_peers[d]) for d in range(7)
-    ]
-
-    def pair_step(n, _):
-        c0 = pl.multiple_of(n * 512, 512)
-        res = f32dot(r2d[...], tmat[:, pl.ds(c0, 512)], ((1,), (0,)))
-        for i in range(4):
-            pbuf[n * 4 + i] = (res[:, i * 128:(i + 1) * 128] + bias[...]).astype(BF)
-        return 0
-
-    lax.fori_loop(0, 4, pair_step, 0)
-    p_cp = pltpu.make_async_copy(pbuf, pair_hbm, s_out.at[0])
-    p_cp.start()
+
+    def w2_copy(n):
+        return link(wzb.at[second], wzb.at[second], w2_s.at[n], w2_r.at[n], second_peer(n))
+
+    w2_cp = [Batch(7, w2_copy)]
+
+    def gl_step(n, _):
+        res = f32dot(wc[...], umat[pl.ds(pl.multiple_of(n * 512, 512), 512), :], ((1,), (1,)))
+        res = res.astype(BF)
+        for c in range(4):
+            gls[n * 4 + c] = res[:, c * 128:(c + 1) * 128]
+        return 0
+
+    lax.fori_loop(0, 2, gl_step, 0)
+
+    def gl_copy(n):
+        c = (col + far(n)) % 8
+        return link(gls.at[c], glr.at[n], gl_s.at[n], gl_r.at[n], (row, c))
+
+    gl_cp = [Batch(7, gl_copy)]
 
     for cp in y_cp:
         cp.wait_recv()
@@ -287,7 +336,13 @@
         acc = grs[mine, c].astype(F32) + gry[0, c].astype(F32) + gry[1, c].astype(F32)
         grz[c] = (acc + gry2[c // 4, c % 4].astype(F32)).astype(BF)
     slot = zl * 2 + ((y - y_src + 8) % 8) // 4
-    o_cp = [send(grz.at[c], gro.at[slot], o_s.at[c], o_r.at[slot], owners[c]) for c in range(8)]
+
+    def o_copy(n):
+        return link(
+            grz.at[n], gro.at[slot], o_s.at[n], o_r.at[slot], (8 * col + 2 * mine + k, n)
+        )
+
+    o_cp = [Batch(8, o_copy)]
 
     for cp in w1_cp + gl_cp + y_cp:
         cp.wait_send()
@@ -306,10 +361,15 @@
     for n in range(1, 4):
         acc = acc + wxb[n].astype(F32)
     wfin[k, first] = acc.astype(BF)
-    w4_cp = [
-        send(wfin.at[k, first], wfin.at[k, first], w4_s.at[d], w4_r.at[d], first_peers[d])
-        for d in range(7)
-    ]
+
+    def w4_copy(n):
+        return link(wfin.at[k, first], wfin.at[k, first], w4_s.at[n], w4_r.at[n], first_peer(n))
+
+    def w5_copy(n):
+        piece = wfin.at[k, (first + 8 - far(n)) % 8]
+        return link(piece, piece, w5_s.at[n + 1], w5_r.at[n + 1], twin)
+
+    w4_cp = [Batch(7, w4_copy)]
     w5_cp = [send(wfin.at[k, first], wfin.at[k, first], w5_s.at[0], w5_r.at[0], twin)]
 
     for cp in gl_cp:
@@ -344,21 +404,16 @@
         cp.wait_send()
     p_cp.wait()
 
-    for d in range(6, -1, -1):
-        w4_cp[d].wait_recv()
-        ys = (first + 8 - FAR[d]) % 8
-        w5_cp.append(
-            send(wfin.at[k, ys], wfin.at[k, ys], w5_s.at[d + 1], w5_r.at[d + 1], twin)
-        )
+    def forward(n, _):
+        w4_copy(6 - n).wait_recv()
+        w5_copy(6 - n).start()
+        return 0
+
+    lax.fori_loop(0, 7, forward, 0)
+    w5_cp.append(Batch(7, w5_copy, start=False))
     for cp in w5_cp:
         cp.wait_recv()
-    for h in range(2):
-        for n in range(8):
-            blk = wfin[h, n].astype(F32) * (8.0 / 65536.0)
-            for tt in range(2):
-                e = h * 16 + n * 2 + tt
-                wg_out[pl.ds(e, 32, stride=32), :] = blk[tt * 32:(tt + 1) * 32]
-    wg_cp = pltpu.make_async_copy(wg_out, wg_hbm, s_out.at[2])
+    wg_cp = pltpu.make_async_copy(wfin, wfin_hbm, s_out.at[2])
     wg_cp.start()
     s_cp.wait()
     for cp in w4_cp + w5_cp:
@@ -366,19 +421,27 @@
     wg_cp.wait()
 
 
-def hand_over(pair, sens, wg, pair_out, sens_out, wg_out, pair_v, sens_v, wg_v, sem_in, sem_out):
-    trips = [(sens, sens_v, sens_out)]
-    for n in range(2):
-        part = pl.ds(n * 512, 512)
-        trips.append((wg.at[part], wg_v.at[part], wg_out.at[part]))
-    for n in range(2):
-        part = pl.ds(n * 8, 8)
-        trips.append((pair.at[part], pair_v.at[part], pair_out.at[part]))
-    ins = [pltpu.make_async_copy(a, b, sem_in.at[n]) for n, (a, b, _) in enumerate(trips)]
-    outs = [pltpu.make_async_copy(b, c, sem_out.at[n]) for n, (_, b, c) in enumerate(trips)]
+def hand_over(
+    pair, sens, wfin, pair_out, sens_out, wg_out, pair_v, sens_v, wfin_v, wg_v, sem_in, sem_out
+):
+    trips = [(wfin, wfin_v), (sens, sens_v)]
+    trips += [(pair.at[pl.ds(n, 2)], pair_v.at[pl.ds(n, 2)]) for n in range(0, 16, 2)]
+    ins = [pltpu.make_async_copy(a, b, sem_in.at[n]) for n, (a, b) in enumerate(trips)]
     for cp in ins:
         cp.start()
-    for a, b in zip(ins, outs):
+    ins[0].wait()
+    trips = [(wg_v.at[pl.ds(n, 256)], wg_out.at[pl.ds(n, 256)]) for n in range(0, 1024, 256)]
+    trips += [(sens_v, sens_out)]
+    trips += [(pair_v.at[pl.ds(n, 2)], pair_out.at[pl.ds(n, 2)]) for n in range(0, 16, 2)]
+    outs = [pltpu.make_async_copy(a, b, sem_out.at[n]) for n, (a, b) in enumerate(trips)]
+    for h in range(2):
+        for n in range(8):
+            blk = wfin_v[h, n].astype(F32) * (8.0 / 65536.0)
+            for tt in range(2):
+                wg_v[pl.ds(h * 16 + n * 2 + tt, 32, stride=32), :] = blk[tt * 32:(tt + 1) * 32]
+    for cp in outs[:4]:
+        cp.start()
+    for a, b in zip(ins[1:], outs[4:]):
         a.wait()
         b.start()
     for cp in outs:
@@ -399,11 +462,11 @@
         ((8, 32, 128), BF), ((8, 32, 128), BF), ((8, 32, 128), BF), ((7, 32, 128), BF),
         ((2, 512, 128), F32), ((2, 512, 128), BF), ((512, 128), BF), ((8, 64, 128), BF),
         ((7, 64, 128), BF), ((8, 64, 128), BF), ((4, 64, 128), BF), ((2, 8, 64, 128), BF),
-        ((16, 128, 128), BF), ((2, 64, 256), BF), ((1024, 128), F32),
+        ((16, 128, 128), BF), ((2, 64, 256), BF),
     ]
     scratch = [pltpu.VMEM(s, d) for s, d in scratch]
     scratch += [dma((5,)), dma((16,)), dma((3,))]
-    for n in (7, 8, 4, 5, 0, 4, 8, 7, 0, 7, 7, 3, 7, 8):
+    for n in (7, 8, 4, 5, 0, 4, 8, 7, 4, 7, 7, 3, 7, 8):
         scratch += [dma((n,)), dma((n,))] if n else [dma, dma]
     shapes = (
         jax.ShapeDtypeStruct((16, 128, 128), BF),
@@ -412,7 +475,7 @@
     )
     results = pl.pallas_call(
         kernel,
-        out_shape=shapes,
+        out_shape=(*shapes[:2], jax.ShapeDtypeStruct((2, 8, 64, 128), BF)),
         in_specs=[anys] * 6,
         out_specs=(anys,) * 3,
         scratch_shapes=scratch,
@@ -425,7 +488,8 @@
         out_shape=shapes,
         in_specs=[anys] * 3,
         out_specs=(anys,) * 3,
-        scratch_shapes=[pltpu.VMEM(o.shape, o.dtype) for o in shapes] + [dma((5,)), dma((5,))],
+        scratch_shapes=[pltpu.VMEM(o.shape, o.dtype) for o in shapes[:2]]
+        + [pltpu.VMEM((2, 8, 64, 128), BF), pltpu.VMEM((1024, 128), F32), dma((10,)), dma((13,))],
     )(*results)
 
 

time: 64.8 us -> 64.7 us (level)
  no operation moved by 1% of the time
where the time goes in v4:
time: 64.7 us; the launch traced here: 64.6 us
  Pallas kernels  63.9 us (99%)
    pallas_call x1, Pallas kernels, on_device(): pl.pallas_call(kernel, out_shape=(*shapes[:2], jax.ShapeDtypeStruct((2, 8...  61.3 us
    pallas_call x1, Pallas kernels, on_device(): pl.pallas_call(hand_over, out_shape=shapes, in_specs=[anys] * 3, out_spec...  2.61 us

profile of v4, /device:TPU:1, one launch (start us, length us, event | category | flops | bytes accessed | tf_op | source)
XLA Modules:
  0.0 64.6 jit_solution(11952231028031401355)
XLA Ops:
  0.6 61.3 %shard_map.85 = (bf16[16,128,128]{2,1,0:T(8,128)(2,1)}, bf16[2,64,256]{2,1,0:T(8,128)(2,1)}, bf16[2,8,64,128]{3,2,1,0:T(8,128)(2,1)}) custom-call(bf16[2,64,256]{2,1,0:T(8,128)(2,1)} %acts_hbm.1, bf16[32,256]{1,0:T(8,128)(2,1)} %bitcast.3, bf16[32,256]{1,0:T(8,128)(2,1)} %bitcast.4, bf16[1024,128]{1,0:T(8,128)(2,1)} %w_hbm.1, f32[1,128]{1,0:T(1,128)} %bitcast.5, ...), custom_call_target="tpu_custom_call" | custom-call | tf_op jit(solution)/shard_map/pallas_call | solution.py:476
  62.0 2.6 %shard_map.86 = (bf16[16,128,128]{2,1,0:T(8,128)(2,1)}, bf16[2,64,256]{2,1,0:T(8,128)(2,1)}, f32[1024,128]{1,0:T(8,128)}) custom-call(bf16[16,128,128]{2,1,0:T(8,128)(2,1)} %get-tuple-element.6.pair, bf16[2,64,256]{2,1,0:T(8,128)(2,1)} %get-tuple-element.7.sens, bf16[2,8,64,128]{3,2,1,0:T(8,128)(2,1)} %get-tuple-element.8.wfin), custom_call_target="tpu_custom_call" | custom-call | tf_op jit(solution)/shard_map/pallas_call | solution.py:486
